TPU v7x, 32 devices: a whole 2x2x4 slice. The times are simulated.
32 devices in a mesh: sample: 4 (over y, x), snp: 8 (over z, core).
Axes of the slice: x: 2, y: 2, z: 4, core: 2. Of those that a mesh axis runs over, the one named last changes fastest.
Arguments:
- dosage: bfloat16 [16384, 16384], P('sample', 'snp'), may hold values from 0 to 2, as said below
- allele_mean: float32 [16384], P('snp'), may hold values from 0.1 to 1.9, as said below
- allele_scale: float32 [16384], P('snp'), may hold values from 1.4 to 3.3, as said below
- probes: float32 [192, 16384], P(None, 'sample'), may hold values from -6 to 6
Outputs:
- applied: float32 [192, 16384], P(None, ('sample', 'snp'))
Inputs may be any that keep to these rules, and one draw needn't show every extreme that they name: dosage holds only the values 0, 1 and 2. allele_mean is twice an allele frequency between 0.05 and 0.95. allele_scale is 1 / sqrt(allele_mean * (1 - allele_mean / 2)).
All inputs are finite; a program needn't handle non-finite values.
Results may differ from a plain program's by a relative error of at most 0.0058.
Values sent between devices are 32-bit elements; how exact they have to be, the bound alone decides.
No kernel may reach another device: no remote copies, remote signals or barrier semaphores. Data moves between devices by JAX's collectives and lax.ppermute only.
A program may use at most 64 MiB of HBM per device.

v0:
```python
import jax
import jax.numpy as jnp
from jax import lax
from jax.sharding import PartitionSpec as P


def on_device(dosage, allele_mean, allele_scale, probes):
    rows = dosage.shape[0]
    total = rows * lax.axis_size("sample")
    width = dosage.shape[1] * lax.axis_size("snp")
    genos = ((dosage.astype(jnp.float32) - allele_mean[None, :]) * allele_scale[None, :]).astype(
        jnp.bfloat16
    )
    probe_b = probes.astype(jnp.bfloat16)
    local = jnp.dot(probe_b, genos, preferred_element_type=jnp.float32)
    loads = lax.psum(local, "sample")
    loads_b = (loads / jnp.sqrt(jnp.float32(total))).astype(jnp.bfloat16)
    partial_rows = lax.dot_general(
        loads_b, genos, (((1,), (1,)), ((), ())), preferred_element_type=jnp.float32
    )
    summed = lax.psum_scatter(partial_rows, "snp", scatter_dimension=1, tiled=True)
    return summed / jnp.sqrt(jnp.float32(width))


def solution(mesh):
    placed = (P("sample", "snp"), P("snp"), P("snp"), P(None, "sample"))
    return jax.shard_map(
        on_device, mesh=mesh, in_specs=placed, out_specs=P(None, ("sample", "snp")), check_vma=False
    )
```

profile of v0, /device:TPU:0, one launch (start us, length us, event | category | flops | bytes accessed | tf_op | source)
XLA Modules:
  0.0 155.6 jit_solution(14594447791897521805)
XLA Ops:
  6.5 0.0 copy-start
  6.5 0.0 copy-start.1
  6.5 0.0 all-reduce.2.cloned.1.call-start
  6.5 13.6 %fusion.2 = f32[192,2048]{0,1:T(8,128)} fusion(bf16[4096,2048]{1,0:T(8,128)(2,1)} %param.4, f32[2048]{0:T(1024)} %param.6, f32[2048]{0:T(1024)} %param.5, f32[192,4096]{1,0:T(8,128)} %param.7), kind=kOutput, calls=%fused_computation.3 | convolution fusion | flops 3255566336 | bytes 21512192 | tf_op jit(solution)/shard_map/dot_general | solution.py:15
  20.1 0.0 all-reduce.2.cloned.1.call-update
  20.2 0.0 reduce-scatter.2.cloned.1.call-start
  20.2 72.4 %all-reduce.2.cloned.1.call-done = f32[192,2048]{0,1:T(8,128)} async-done(((f32[192,2048]{0,1:T(8,128)}), f32[192,2048]{0,1:T(8,128)}) %all-reduce.2.cloned.1.call-update) | async-done | bytes 1572880 | tf_op jit(solution)/shard_map/psum | solution.py:16
  92.6 0.0 copy-done
  92.6 0.0 copy-done.1
  92.6 13.8 %fusion = f32[192,4096]{1,0:T(8,128)} fusion(bf16[4096,2048]{1,0:T(8,128)(2,1)} %param.4, f32[2048]{0:T(1024)S(1)} %copy-done, f32[2048]{0:T(1024)S(1)} %copy-done.1, f32[192,2048]{0,1:T(8,128)} %all-reduce.2.cloned.1.call-done), kind=kOutput, calls=%fused_computation.1 | convolution fusion | flops 3255566336 | bytes 21512192 | tf_op jit(solution)/shard_map/dot_general | solution.py:18
  106.5 0.0 reduce-scatter.2.cloned.1.call-update
  106.5 40.5 %reduce-scatter.2.cloned.1.call-done = f32[192,512]{1,0:T(8,128)} async-done(((f32[192,4096]{1,0:T(8,128)}), f32[192,512]{1,0:T(8,128)}) %reduce-scatter.2.cloned.1.call-update) | async-done | bytes 393232 | tf_op jit(solution)/shard_map/reduce_scatter | solution.py:21
  147.0 1.8 %broadcast_multiply_fusion = f32[192,512]{1,0:T(8,128)} fusion(f32[192,512]{1,0:T(8,128)} %reduce-scatter.2.cloned.1.call-done), kind=kLoop, calls=%fused_computation.7 | loop fusion | flops 98304 | bytes 786432 | tf_op jit(solution)/shard_map/div | solution.py:22
Async XLA Ops:
  6.5 86.1 %copy-start = (f32[2048]{0:T(1024)S(1)}, f32[2048]{0:T(1024)}, u32[]{:S(2)}) copy-start(f32[2048]{0:T(1024)} %param.6) | copy-start | bytes 24580
  6.5 86.1 %copy-start.1 = (f32[2048]{0:T(1024)S(1)}, f32[2048]{0:T(1024)}, u32[]{:S(2)}) copy-start(f32[2048]{0:T(1024)} %param.5) | copy-start | bytes 24580
  6.5 86.1 %all-reduce.2.cloned.1.call-start = ((), (), s32[]{:S(2)}) async-start(), calls=%async_computation.1 | async-start | bytes 4194304 | tf_op jit(solution)/shard_map/psum | solution.py:16
  20.2 126.8 %reduce-scatter.2.cloned.1.call-start = ((), (), s32[]{:S(2)}) async-start(), calls=%async_computation.2 | async-start | bytes 3538944 | tf_op jit(solution)/shard_map/reduce_scatter | solution.py:21
Sparse Core Ops, SparseCore 0:
  20.3 72.3 all-reduce.1
  106.6 40.3 reduce-scatter.1
where the time goes:
time: 156 us
  waiting for transfers between devices  113 us (72%)
  matrix products  27.4 us (18%)
  between operations  13.4 us (9%)
  other arithmetic  1.77 us (1%)
    psum x1, waiting for transfers between devices, on_device(): loads = lax.psum(local, 'sample')  72.4 us
    reduce_scatter x1, waiting for transfers between devices, on_device(): lax.psum_scatter(partial_rows, 'snp', scatter_dimension=1, tiled=True)  40.5 us
    dot_general x1, matrix products, on_device(): lax.dot_general(loads_b, genos, (((1,), (1,)), ((), ())), preferred_eleme...  13.8 us
    dot_general x1, matrix products, on_device(): local = jnp.dot(probe_b, genos, preferred_element_type=jnp.float32)  13.6 us
  transfers between devices with their start and end apart: 2, of which 2 were waited for; matrix products, arithmetic and copies ran while one was open for 0% of the time, Pallas kernels for 0%

commit v1 on v0

--- a/solution.py
+++ b/solution.py
@@ -1,10 +1,229 @@
+import functools
+
 import jax
 import jax.numpy as jnp
 from jax import lax
+from jax.experimental import pallas as pl
+from jax.experimental.pallas import tpu as pltpu
 from jax.sharding import PartitionSpec as P
 
-
-def on_device(dosage, allele_mean, allele_scale, probes):
+AXES = ("sample", "snp")
+CHUNKS = (96, 96)
+STEPS = 8
+LIMIT = 20 * 1024 * 1024
+VMEM = pl.BlockSpec(memory_space=pltpu.VMEM)
+SMEM = pl.BlockSpec(memory_space=pltpu.SMEM)
+HBM = pl.BlockSpec(memory_space=pltpu.HBM)
+F32 = jnp.float32
+LIGHT = pl.CostEstimate(flops=1, bytes_accessed=1, transcendentals=0)
+
+
+def pairs(move):
+    found = []
+    for index in range(32):
+        y, x, z, core = index // 16, index // 8 % 2, index // 2 % 4, index % 2
+        y, x, z, core = move(y, x, z, core)
+        found.append((index, y * 16 + x * 8 + z * 2 + core))
+    return found
+
+
+PLANE_FIRST = pairs(lambda y, x, z, c: (y, 1 - x, z, c) if c == 0 else (1 - y, x, z, c))
+PLANE_SECOND = pairs(lambda y, x, z, c: (1 - y, x, z, c) if c == 0 else (y, 1 - x, z, c))
+CORES = pairs(lambda y, x, z, c: (y, x, z, 1 - c))
+LINE_FIRST = pairs(lambda y, x, z, c: (y, x, z ^ (1 if c == 0 else 2), c))
+LINE_SECOND = pairs(lambda y, x, z, c: (y, x, z ^ (2 if c == 0 else 1), c))
+
+
+def loads_kernel(first, place, probes, dosage, mean, *refs):
+    count = len(CHUNKS)
+    if first:
+        parts, (probe_b, sums, held, wide, middles, sem, sem_p, sem_m) = refs[:count], refs[count:]
+    else:
+        sums_in, parts, (held, sem) = refs[0], refs[2 : 2 + count], refs[2 + count :]
+    slot = 0 if first else 1
+    _, rows, width = held.shape
+    block = rows // STEPS
+    half = 1 - place[0] if first else place[0]
+    start = pl.multiple_of(half * width, width)
+
+    def copies(step):
+        at = pl.ds(step * block, block)
+        made = [pltpu.make_async_copy(dosage.at[at, pl.ds(start, width)], held.at[slot, at], sem.at[step])]
+        if first:
+            made.append(pltpu.make_async_copy(probes.at[:, at], wide.at[:, at], sem_p.at[step]))
+        return made
+
+    for step in range(STEPS):
+        for copy in copies(step):
+            copy.start()
+    if first:
+        copy_mean = pltpu.make_async_copy(mean, middles, sem_m)
+        copy_mean.start()
+    for step in range(STEPS):
+        at = pl.ds(step * block, block)
+        for copy in copies(step):
+            copy.wait()
+        if first:
+            left = wide[:, at].astype(jnp.bfloat16)
+            probe_b[:, at] = left
+            share = jnp.sum(left.astype(F32), axis=1, keepdims=True)
+            total = share if step == 0 else total + share
+        else:
+            left = probes[:, at]
+        right = held[slot, at]
+        low = 0
+        for part, many in zip(parts, CHUNKS):
+            product = jnp.dot(left[low : low + many], right, preferred_element_type=F32)
+            if step == 0:
+                part[...] = product
+            else:
+                part[...] += product
+            low += many
+    if first:
+        sums[...] = jnp.broadcast_to(total, sums.shape)
+        copy_mean.wait()
+        middle = middles[:, pl.ds(start, width)]
+    else:
+        total = sums_in[:, :1]
+        middle = mean[:, pl.ds(start, width)]
+    low = 0
+    for part, many in zip(parts, CHUNKS):
+        part[...] -= total[low : low + many] * middle
+        low += many
+
+
+def in_hbm(*arrays):
+    return [pltpu.with_memory_space_constraint(array, pltpu.HBM) for array in arrays]
+
+
+def in_vmem(*arrays):
+    return [pltpu.with_memory_space_constraint(array, pltpu.VMEM) for array in arrays]
+
+
+def first_half(place, probes, dosage, mean):
+    count, rows = probes.shape
+    width = dosage.shape[1] // 2
+    return pl.pallas_call(
+        functools.partial(loads_kernel, True),
+        in_specs=[SMEM, HBM, HBM, HBM],
+        out_specs=[VMEM] * (len(CHUNKS) + 3),
+        out_shape=[jax.ShapeDtypeStruct((many, width), F32) for many in CHUNKS]
+        + [
+            jax.ShapeDtypeStruct((count, rows), jnp.bfloat16),
+            jax.ShapeDtypeStruct((count, 128), F32),
+            pltpu.VMEM((2, rows, width), jnp.bfloat16),
+        ],
+        scratch_shapes=[
+            pltpu.VMEM((count, rows), F32),
+            pltpu.VMEM((1, 2 * width), F32),
+            pltpu.SemaphoreType.DMA((STEPS,)),
+            pltpu.SemaphoreType.DMA((STEPS,)),
+            pltpu.SemaphoreType.DMA,
+        ],
+        compiler_params=pltpu.CompilerParams(vmem_limit_bytes=LIMIT),
+        cost_estimate=LIGHT,
+        name="loads_sent",
+    )(place, *in_hbm(probes, dosage, mean))
+
+
+def second_half(place, probe_b, dosage, mean, sums, held):
+    count, rows = probe_b.shape
+    width = dosage.shape[1] // 2
+    return pl.pallas_call(
+        functools.partial(loads_kernel, False),
+        in_specs=[SMEM, VMEM, HBM, VMEM, VMEM, VMEM],
+        out_specs=[VMEM] * (len(CHUNKS) + 1),
+        out_shape=[jax.ShapeDtypeStruct((many, width), F32) for many in CHUNKS]
+        + [pltpu.VMEM((2, rows, width), jnp.bfloat16)],
+        scratch_shapes=[pltpu.SemaphoreType.DMA((STEPS,))],
+        input_output_aliases={5: len(CHUNKS)},
+        compiler_params=pltpu.CompilerParams(vmem_limit_bytes=LIMIT),
+        cost_estimate=LIGHT,
+        name="loads_kept",
+    )(place, probe_b, *in_hbm(dosage), mean, sums, *in_vmem(held))
+
+
+def apply_kernel(first, factor, shrink, place, *refs):
+    if first:
+        own, other, mean, scale, held, sent, kept, left_out, shift_out = refs
+        half = place[0]
+        width = own.shape[1]
+        lefts, shift = [], 0.0
+        for slot, ref, at in ((0, other, 1 - half), (1, own, half)):
+            span = pl.ds(pl.multiple_of(at * width, width), width)
+            gain = scale[:, span]
+            left = (ref[...] * (gain * gain * factor)).astype(jnp.bfloat16)
+            shift = shift + jnp.sum(left.astype(F32) * mean[:, span], axis=1, keepdims=True)
+            left_out[slot] = left
+            lefts.append(left)
+        shift = shift * shrink
+        shift_out[...] = jnp.broadcast_to(shift, shift_out.shape)
+    else:
+        left_in, shift_in, held, sent, kept = refs
+        lefts = [left_in[0], left_in[1]]
+        shift = shift_in[:, :1]
+    core, z = place[1], place[2]
+    block = held.shape[1] // 8
+    mask = 1 + core
+    for out, one, two, owner in ((sent, mask, 3 - mask, 1 - core), (kept, 3 - mask, mask, core)):
+        for index, flip in enumerate((two, 3) if first else (0, one)):
+            at = pl.ds(pl.multiple_of(((z ^ flip) * 2 + owner) * block, block), block)
+            product = 0.0
+            for slot, left in enumerate(lefts):
+                product = product + lax.dot_general(
+                    left, held[slot, at], (((1,), (1,)), ((), ())), preferred_element_type=F32
+                )
+            out[:, index * block : (index + 1) * block] = product * shrink - shift
+
+
+def apply_rows(first, factor, shrink, place, *arrays):
+    many = arrays[0].shape[-2]
+    held = arrays[-1]
+    wide = held.shape[1] // 4
+    out_shape = [jax.ShapeDtypeStruct((many, wide), F32)] * 2
+    if first:
+        out_shape += [
+            jax.ShapeDtypeStruct((2, many, held.shape[2]), jnp.bfloat16),
+            jax.ShapeDtypeStruct((many, 128), F32),
+        ]
+    return pl.pallas_call(
+        functools.partial(apply_kernel, first, factor, shrink),
+        in_specs=[SMEM] + [VMEM] * len(arrays),
+        out_specs=[VMEM] * len(out_shape),
+        out_shape=out_shape,
+        compiler_params=pltpu.CompilerParams(vmem_limit_bytes=LIMIT),
+        cost_estimate=LIGHT,
+        name="apply_first" if first else "apply_second",
+    )(place, *arrays[:-1], *in_vmem(held))
+
+
+def on_slice(dosage, allele_mean, allele_scale, probes):
+    total = dosage.shape[0] * lax.axis_size("sample")
+    across = dosage.shape[1] * lax.axis_size("snp")
+    sample, snp = lax.axis_index("sample"), lax.axis_index("snp")
+    core, z = snp % 2, snp // 2
+    half = jnp.where(core == 0, sample % 2, sample // 2)
+    place = jnp.stack([half, core, z]).astype(jnp.int32)
+    mean, scale = allele_mean[None, :], allele_scale[None, :]
+    *sent, probe_b, sums, held = first_half(place, probes, dosage, mean)
+    *kept, held = second_half(place, probe_b, dosage, mean, sums, held)
+    factor, shrink = total**-0.5, across**-0.5
+    results = []
+    for part, own in zip(sent, kept):
+        own = own + lax.ppermute(part, AXES, PLANE_FIRST)
+        own = own + lax.ppermute(own, AXES, PLANE_SECOND)
+        other = lax.ppermute(own, AXES, PLANE_FIRST)
+        sent_a, kept_a, left, shift = apply_rows(True, factor, shrink, place, own, other, mean, scale, held)
+        sent_b, kept_b = apply_rows(False, factor, shrink, place, left, shift, held)
+        kept_a = kept_a + lax.ppermute(sent_a, AXES, CORES)
+        kept_b = kept_b + lax.ppermute(sent_b, AXES, CORES)
+        kept_b = kept_b + lax.ppermute(kept_a, AXES, LINE_FIRST)
+        width = kept_b.shape[1] // 2
+        results.append(kept_b[:, :width] + lax.ppermute(kept_b[:, width:], AXES, LINE_SECOND))
+    return jnp.concatenate(results, axis=0)
+
+
+def on_any(dosage, allele_mean, allele_scale, probes):
     rows = dosage.shape[0]
     total = rows * lax.axis_size("sample")
     width = dosage.shape[1] * lax.axis_size("snp")
@@ -24,6 +243,7 @@
 
 def solution(mesh):
     placed = (P("sample", "snp"), P("snp"), P("snp"), P(None, "sample"))
+    body = on_slice if (mesh.shape["sample"], mesh.shape["snp"]) == (4, 8) else on_any
     return jax.shard_map(
-        on_device, mesh=mesh, in_specs=placed, out_specs=P(None, ("sample", "snp")), check_vma=False
+        body, mesh=mesh, in_specs=placed, out_specs=P(None, ("sample", "snp")), check_vma=False
     )

time: 156 us -> 81.2 us (0.52)
  waiting for transfers between devices: 113 us -> 33.9 us
  matrix products: 27.4 us -> 0 us
  Pallas kernels: 0 us -> 23.3 us
  starting transfers between devices: 0.04 us -> 22.3 us
  between operations: 13.4 us -> 0.13 us
    psum x1 -> x0, waiting for transfers between devices: 72.4 us -> none  [on_device(): loads = lax.psum(local, 'sample')]
    reduce_scatter x1 -> x0, waiting for transfers between devices: 40.5 us -> none  [on_device(): lax.psum_scatter(partial_rows, 'snp', scatter_dimension=1, tiled=True)]
    ppermute x0 -> x14, waiting for transfers between devices: none -> 33.9 us  [the longest x2 13.3 us: on_slice(): kept_b = kept_b + lax.ppermute(kept_a, AXES, LINE_FIRST)]
    dot_general x2 -> x0, matrix products: 27.4 us -> none  [the longest x1 13.8 us: on_device(): lax.dot_general(loads_b, genos, (((1,), (1,)), ((), ())), preferred_eleme...]
    pallas_call x0 -> x6, Pallas kernels: none -> 23.3 us  [the longest x4 12.9 us: apply_rows(): pl.pallas_call(functools.partial(apply_kernel, first, factor, shrink), in...]
    ppermute x0 -> x14, starting transfers between devices: none -> 22.3 us  [the longest x2 5.37 us: on_slice(): lax.ppermute(kept_b[:, width:], AXES, LINE_SECOND)]
    div x1 -> x0, other arithmetic: 1.77 us -> none  [on_device(): return summed / jnp.sqrt(jnp.float32(width))]
  transfers between devices with their start and end apart: 2 -> 14, of which waited for: 2 -> 7; matrix products, arithmetic and copies ran while one was open for 0% -> 1% of each run, Pallas kernels for 0% -> 22%
where the time goes in v1:
time: 81.2 us; the launch traced here: 81 us
  waiting for transfers between devices  33.9 us (42%)
  Pallas kernels  23.3 us (29%)
  starting transfers between devices  22.3 us (27%)
  other arithmetic  1.35 us (2%)
    ppermute x2, waiting for transfers between devices, on_slice(): kept_b = kept_b + lax.ppermute(kept_a, AXES, LINE_FIRST)  13.3 us
    pallas_call x4, Pallas kernels, apply_rows(): pl.pallas_call(functools.partial(apply_kernel, first, factor, shrink), in...  12.9 us
    ppermute x2, waiting for transfers between devices, on_slice(): own = own + lax.ppermute(own, AXES, PLANE_SECOND)  7.45 us
    ppermute x2, waiting for transfers between devices, on_slice(): lax.ppermute(kept_b[:, width:], AXES, LINE_SECOND)  5.67 us
    pallas_call x1, Pallas kernels, first_half(): pl.pallas_call(functools.partial(loads_kernel, True), in_specs=[SMEM, HBM...  5.5 us
    ppermute x2, starting transfers between devices, on_slice(): lax.ppermute(kept_b[:, width:], AXES, LINE_SECOND)  5.37 us
    ppermute x2, waiting for transfers between devices, on_slice(): own = own + lax.ppermute(part, AXES, PLANE_FIRST)  5.02 us
    pallas_call x1, Pallas kernels, second_half(): pl.pallas_call(functools.partial(loads_kernel, False), in_specs=[SMEM, VM...  4.86 us
  transfers between devices with their start and end apart: 14, of which 7 were waited for; matrix products, arithmetic and copies ran while one was open for 1% of the time, Pallas kernels for 22%

profile of v1, /device:TPU:0, one launch (start us, length us, event | category | flops | bytes accessed | tf_op | source)
XLA Modules:
  0.0 81.0 jit_solution(1338158223518165437)
XLA Ops:
  0.0 0.1 pad_add_fusion.place
  0.1 5.5 %loads_sent.1 = (f32[96,1024]{1,0:T(8,128)S(1)}, f32[96,1024]{1,0:T(8,128)S(1)}, bf16[192,4096]{1,0:T(8,128)(2,1)S(1)}, f32[192,128]{1,0:T(8,128)S(1)}, bf16[2,4096,1024]{2,1,0:T(8,128)(2,1)S(1)}) custom-call(s32[3]{0:T(128)S(1)} %pad_add_fusion.place, f32[192,4096]{1,0:T(8,128)} %probes.1, bf16[4096,2048]{1,0:T(8,128)(2,1)} %dosage.3, f32[1,2048]{1,0:T(1,128)} %bitcast.5), custom_call_target="tpu_custom_call" | custom-call | flops 1 | bytes 1 | tf_op jit(solution)/shard_map/loads_sent/pallas_call | solution.py:106
  5.6 3.0 %collective-permute-start.7 = (f32[96,1024]{1,0:T(8,128)S(1)}, f32[96,1024]{1,0:T(8,128)S(1)}, u32[]{:S(2)}, u32[]{:S(2)}) collective-permute-start(f32[96,1024]{1,0:T(8,128)S(1)} %get-tuple-element.38), channel_id=1, source_target_pairs={{0,8},{1,17},{2,10},{3,19},{4,12},{5,21},{6,14},{7,23},{8,0},{9,25... | collective-permute-start | bytes 1179656 | tf_op jit(solution)/shard_map/ppermute | solution.py:213
  8.6 0.1 collective-permute-start
  8.7 4.9 %loads_kept.1 = (f32[96,1024]{1,0:T(8,128)S(1)}, f32[96,1024]{1,0:T(8,128)S(1)}, bf16[2,4096,1024]{2,1,0:T(8,128)(2,1)S(1)}) custom-call(s32[3]{0:T(128)S(1)} %pad_add_fusion.place, bf16[192,4096]{1,0:T(8,128)(2,1)S(1)} %get-tuple-element.25.probes, bf16[4096,2048]{1,0:T(8,128)(2,1)} %dosage.3, ...), custom_call_target="tpu_custom_call", output_to_operand_aliasing={{2}: (5, {})} | custom-call | flops 1 | bytes 1 | tf_op jit(solution)/shard_map/loads_kept/pallas_call | solution.py:132
  13.5 0.8 collective-permute-done.7
  14.4 2.1 %collective-permute-start.8 = (f32[96,1024]{1,0:T(8,128)S(1)}, f32[96,1024]{1,0:T(8,128)S(1)}, u32[]{:S(2)}, u32[]{:S(2)}) collective-permute-start(f32[96,1024]{1,0:T(8,128)S(1)} %add.53), channel_id=1, source_target_pairs={{0,16},{1,9},{2,18},{3,11},{4,20},{5,13},{6,22},{7,15},{8,24},{9,1... | collective-permute-start | bytes 1179656 | tf_op jit(solution)/shard_map/ppermute | solution.py:214
  16.5 4.2 %collective-permute-done = f32[96,1024]{1,0:T(8,128)S(1)} collective-permute-done((f32[96,1024]{1,0:T(8,128)S(1)}, f32[96,1024]{1,0:T(8,128)S(1)}, u32[]{:S(2)}, u32[]{:S(2)}) %collective-permute-start) | collective-permute-done | bytes 393248 | tf_op jit(solution)/shard_map/ppermute | solution.py:213
  20.8 2.4 %collective-permute-start.1 = (f32[96,1024]{1,0:T(8,128)S(1)}, f32[96,1024]{1,0:T(8,128)S(1)}, u32[]{:S(2)}, u32[]{:S(2)}) collective-permute-start(f32[96,1024]{1,0:T(8,128)S(1)} %add.47), channel_id=1, source_target_pairs={{0,16},{1,9},{2,18},{3,11},{4,20},{5,13},{6,22},{7,15},{8,24},{9,1... | collective-permute-start | bytes 1179656 | tf_op jit(solution)/shard_map/ppermute | solution.py:214
  23.2 0.1 add.54.refs_0_
  23.2 1.6 %collective-permute-start.9 = (f32[96,1024]{1,0:T(8,128)S(1)}, f32[96,1024]{1,0:T(8,128)S(1)}, u32[]{:S(2)}, u32[]{:S(2)}) collective-permute-start(f32[96,1024]{1,0:T(8,128)S(1)} %add.54.refs_0_), channel_id=1, source_target_pairs={{0,8},{1,17},{2,10},{3,19},{4,12},{5,21},{6,14},{7,23},{8,0},{9,25... | collective-permute-start | bytes 1179656 | tf_op jit(solution)/shard_map/ppermute | solution.py:215
  24.8 7.4 %collective-permute-done.1 = f32[96,1024]{1,0:T(8,128)S(1)} collective-permute-done((f32[96,1024]{1,0:T(8,128)S(1)}, f32[96,1024]{1,0:T(8,128)S(1)}, u32[]{:S(2)}, u32[]{:S(2)}) %collective-permute-start.1) | collective-permute-done | bytes 393248 | tf_op jit(solution)/shard_map/ppermute | solution.py:214
  32.3 2.4 %collective-permute-start.2 = (f32[96,1024]{1,0:T(8,128)S(1)}, f32[96,1024]{1,0:T(8,128)S(1)}, u32[]{:S(2)}, u32[]{:S(2)}) collective-permute-start(f32[96,1024]{1,0:T(8,128)S(1)} %add.48.refs_0_), channel_id=1, source_target_pairs={{0,8},{1,17},{2,10},{3,19},{4,12},{5,21},{6,14},{7,23},{8,0},{9,25... | collective-permute-start | bytes 1179656 | tf_op jit(solution)/shard_map/ppermute | solution.py:215
  34.7 3.3 %apply_first.3 = (f32[96,1024]{1,0:T(8,128)S(1)}, f32[96,1024]{1,0:T(8,128)S(1)}, bf16[2,96,1024]{2,1,0:T(8,128)(2,1)S(1)}, f32[96,128]{1,0:T(8,128)S(1)}) custom-call(s32[3]{0:T(128)S(1)} %pad_add_fusion.place, f32[96,1024]{1,0:T(8,128)S(1)} %add.54.refs_0_, f32[96,1024]{1,0:T(8,128)S(1)} %collective-permute-done.9.refs_1_, f32[1,2048]{1,0:T(1,128)S(1)} %bitcast.7, ...), custom_call_target="tpu_custom_call" | custom-call | flops 1 | bytes 1 | tf_op jit(solution)/shard_map/apply_first/pallas_call | solution.py:189
  38.0 0.1 collective-permute-start.11
  38.1 2.4 %collective-permute-done.2.refs_1_ = f32[96,1024]{1,0:T(8,128)S(1)} collective-permute-done((f32[96,1024]{1,0:T(8,128)S(1)}, f32[96,1024]{1,0:T(8,128)S(1)}, u32[]{:S(2)}, u32[]{:S(2)}) %collective-permute-start.2) | collective-permute-done | bytes 393248 | tf_op jit(solution)/shard_map/ppermute | solution.py:215
  40.5 3.3 %apply_first.2 = (f32[96,1024]{1,0:T(8,128)S(1)}, f32[96,1024]{1,0:T(8,128)S(1)}, bf16[2,96,1024]{2,1,0:T(8,128)(2,1)S(1)}, f32[96,128]{1,0:T(8,128)S(1)}) custom-call(s32[3]{0:T(128)S(1)} %pad_add_fusion.place, f32[96,1024]{1,0:T(8,128)S(1)} %add.48.refs_0_, f32[96,1024]{1,0:T(8,128)S(1)} %collective-permute-done.2.refs_1_, f32[1,2048]{1,0:T(1,128)S(1)} %bitcast.8, ...), custom_call_target="tpu_custom_call" | custom-call | flops 1 | bytes 1 | tf_op jit(solution)/shard_map/apply_first/pallas_call | solution.py:189
  43.7 0.1 collective-permute-start.4
  43.8 3.2 %apply_second.3 = (f32[96,1024]{1,0:T(8,128)S(1)}, f32[96,1024]{1,0:T(8,128)S(1)}) custom-call(s32[3]{0:T(128)S(1)} %pad_add_fusion.place, bf16[2,96,1024]{2,1,0:T(8,128)(2,1)S(1)} %get-tuple-element.39.refs_0_, f32[96,128]{1,0:T(8,128)S(1)} %get-tuple-element.40.refs_1_, bf16[2,4096,1024]{2,1,0:T(8,128)(2,1)S(1)} %get-tuple-element.30.refs_4_.refs_2_), custom_call_target="tpu_custom_call" | custom-call | flops 1 | bytes 1 | tf_op jit(solution)/shard_map/apply_second/pallas_call | solution.py:189
  47.0 0.6 collective-permute-start.10
  47.7 2.2 %collective-permute-start.12 = (f32[96,1024]{1,0:T(8,128)S(1)}, f32[96,1024]{1,0:T(8,128)S(1)}, u32[]{:S(2)}, u32[]{:S(2)}) collective-permute-start(f32[96,1024]{1,0:T(8,128)S(1)} %add.56), channel_id=1, source_target_pairs={{0,2},{1,5},{2,0},{3,7},{4,6},{5,1},{6,4},{7,3},{8,10},{9,13},{10,... | collective-permute-start | bytes 1179656 | tf_op jit(solution)/shard_map/ppermute | solution.py:220
  49.8 3.2 %apply_second.2 = (f32[96,1024]{1,0:T(8,128)S(1)}, f32[96,1024]{1,0:T(8,128)S(1)}) custom-call(s32[3]{0:T(128)S(1)} %pad_add_fusion.place, bf16[2,96,1024]{2,1,0:T(8,128)(2,1)S(1)} %get-tuple-element.31.refs_0_, f32[96,128]{1,0:T(8,128)S(1)} %get-tuple-element.32.refs_1_, bf16[2,4096,1024]{2,1,0:T(8,128)(2,1)S(1)} %get-tuple-element.30.refs_4_.refs_2_), custom_call_target="tpu_custom_call" | custom-call | flops 1 | bytes 1 | tf_op jit(solution)/shard_map/apply_second/pallas_call | solution.py:189
  53.0 0.8 %collective-permute-start.3 = (f32[96,1024]{1,0:T(8,128)S(1)}, f32[96,1024]{1,0:T(8,128)S(1)}, u32[]{:S(2)}, u32[]{:S(2)}) collective-permute-start(f32[96,1024]{1,0:T(8,128)S(1)} %get-tuple-element.34), channel_id=1, source_target_pairs={{0,1},{1,0},{2,3},{3,2},{4,5},{5,4},{6,7},{7,6},{8,9},{9,8},{10,11... | collective-permute-start | bytes 1179656 | tf_op jit(solution)/shard_map/ppermute | solution.py:219
  53.9 1.6 %collective-permute-start.5 = (f32[96,1024]{1,0:T(8,128)S(1)}, f32[96,1024]{1,0:T(8,128)S(1)}, u32[]{:S(2)}, u32[]{:S(2)}) collective-permute-start(f32[96,1024]{1,0:T(8,128)S(1)} %add.50), channel_id=1, source_target_pairs={{0,2},{1,5},{2,0},{3,7},{4,6},{5,1},{6,4},{7,3},{8,10},{9,13},{10,... | collective-permute-start | bytes 1179656 | tf_op jit(solution)/shard_map/ppermute | solution.py:220
  55.6 3.9 %collective-permute-done.12 = f32[96,1024]{1,0:T(8,128)S(1)} collective-permute-done((f32[96,1024]{1,0:T(8,128)S(1)}, f32[96,1024]{1,0:T(8,128)S(1)}, u32[]{:S(2)}, u32[]{:S(2)}) %collective-permute-start.12) | collective-permute-done | bytes 393248 | tf_op jit(solution)/shard_map/ppermute | solution.py:220
  59.4 0.1 add_add_fusion
  59.5 3.5 %collective-permute-start.13 = (f32[96,512]{1,0:T(8,128)S(1)}, f32[96,512]{1,0:T(8,128)S(1)}, u32[]{:S(2)}, u32[]{:S(2)}) collective-permute-start(f32[96,512]{1,0:T(8,128)S(1)} %slice.19), channel_id=1, source_target_pairs={{0,4},{1,3},{2,6},{3,1},{4,0},{5,7},{6,2},{7,5},{8,12},{9,11},{10,... | collective-permute-start | bytes 589832 | tf_op jit(solution)/shard_map/ppermute | solution.py:222
  63.0 9.4 %collective-permute-done.5 = f32[96,1024]{1,0:T(8,128)S(1)} collective-permute-done((f32[96,1024]{1,0:T(8,128)S(1)}, f32[96,1024]{1,0:T(8,128)S(1)}, u32[]{:S(2)}, u32[]{:S(2)}) %collective-permute-start.5) | collective-permute-done | bytes 393248 | tf_op jit(solution)/shard_map/ppermute | solution.py:220
  72.4 0.1 add_add_fusion.1
  72.5 1.9 %collective-permute-start.6 = (f32[96,512]{1,0:T(8,128)S(1)}, f32[96,512]{1,0:T(8,128)S(1)}, u32[]{:S(2)}, u32[]{:S(2)}) collective-permute-start(f32[96,512]{1,0:T(8,128)S(1)} %slice.17), channel_id=1, source_target_pairs={{0,4},{1,3},{2,6},{3,1},{4,0},{5,7},{6,2},{7,5},{8,12},{9,11},{10,... | collective-permute-start | bytes 589832 | tf_op jit(solution)/shard_map/ppermute | solution.py:222
  74.5 5.7 %collective-permute-done.6 = f32[96,512]{1,0:T(8,128)S(1)} collective-permute-done((f32[96,512]{1,0:T(8,128)S(1)}, f32[96,512]{1,0:T(8,128)S(1)}, u32[]{:S(2)}, u32[]{:S(2)}) %collective-permute-start.6) | collective-permute-done | bytes 196640 | tf_op jit(solution)/shard_map/ppermute | solution.py:222
  80.2 0.8 pad_maximum_fusion
  (20 shorter events, 0.3 us)
Async XLA Ops:
  0.0 8.7 %copy-start = (f32[2048]{0:T(1024)S(1)}, f32[2048]{0:T(1024)}, u32[]{:S(2)}) copy-start(f32[2048]{0:T(1024)} %param.5) | copy-start | bytes 24580
  5.6 8.8 %collective-permute-start.7 = (f32[96,1024]{1,0:T(8,128)S(1)}, f32[96,1024]{1,0:T(8,128)S(1)}, u32[]{:S(2)}, u32[]{:S(2)}) collective-permute-start(f32[96,1024]{1,0:T(8,128)S(1)} %get-tuple-element.38), channel_id=1, source_target_pairs={{0,8},{1,17},{2,10},{3,19},{4,12},{5,21},{6,14},{7,23},{8,0},{9,25... | collective-permute-start | bytes 1179656 | tf_op jit(solution)/shard_map/ppermute | solution.py:213
  8.6 12.1 %collective-permute-start = (f32[96,1024]{1,0:T(8,128)S(1)}, f32[96,1024]{1,0:T(8,128)S(1)}, u32[]{:S(2)}, u32[]{:S(2)}) collective-permute-start(f32[96,1024]{1,0:T(8,128)S(1)} %get-tuple-element.29), channel_id=1, source_target_pairs={{0,8},{1,17},{2,10},{3,19},{4,12},{5,21},{6,14},{7,23},{8,0},{9,25... | collective-permute-start | bytes 1179656 | tf_op jit(solution)/shard_map/ppermute | solution.py:213
  8.7 26.0 %copy-start.1 = (f32[2048]{0:T(1024)S(1)}, f32[2048]{0:T(1024)}, u32[]{:S(2)}) copy-start(f32[2048]{0:T(1024)} %param.6) | copy-start | bytes 24580
  14.4 8.8 %collective-permute-start.8 = (f32[96,1024]{1,0:T(8,128)S(1)}, f32[96,1024]{1,0:T(8,128)S(1)}, u32[]{:S(2)}, u32[]{:S(2)}) collective-permute-start(f32[96,1024]{1,0:T(8,128)S(1)} %add.53), channel_id=1, source_target_pairs={{0,16},{1,9},{2,18},{3,11},{4,20},{5,13},{6,22},{7,15},{8,24},{9,1... | collective-permute-start | bytes 1179656 | tf_op jit(solution)/shard_map/ppermute | solution.py:214
  20.8 11.5 %collective-permute-start.1 = (f32[96,1024]{1,0:T(8,128)S(1)}, f32[96,1024]{1,0:T(8,128)S(1)}, u32[]{:S(2)}, u32[]{:S(2)}) collective-permute-start(f32[96,1024]{1,0:T(8,128)S(1)} %add.47), channel_id=1, source_target_pairs={{0,16},{1,9},{2,18},{3,11},{4,20},{5,13},{6,22},{7,15},{8,24},{9,1... | collective-permute-start | bytes 1179656 | tf_op jit(solution)/shard_map/ppermute | solution.py:214
  23.2 11.5 %collective-permute-start.9 = (f32[96,1024]{1,0:T(8,128)S(1)}, f32[96,1024]{1,0:T(8,128)S(1)}, u32[]{:S(2)}, u32[]{:S(2)}) collective-permute-start(f32[96,1024]{1,0:T(8,128)S(1)} %add.54.refs_0_), channel_id=1, source_target_pairs={{0,8},{1,17},{2,10},{3,19},{4,12},{5,21},{6,14},{7,23},{8,0},{9,25... | collective-permute-start | bytes 1179656 | tf_op jit(solution)/shard_map/ppermute | solution.py:215
  32.3 8.2 %collective-permute-start.2 = (f32[96,1024]{1,0:T(8,128)S(1)}, f32[96,1024]{1,0:T(8,128)S(1)}, u32[]{:S(2)}, u32[]{:S(2)}) collective-permute-start(f32[96,1024]{1,0:T(8,128)S(1)} %add.48.refs_0_), channel_id=1, source_target_pairs={{0,8},{1,17},{2,10},{3,19},{4,12},{5,21},{6,14},{7,23},{8,0},{9,25... | collective-permute-start | bytes 1179656 | tf_op jit(solution)/shard_map/ppermute | solution.py:215
  38.0 9.6 %collective-permute-start.11 = (f32[96,1024]{1,0:T(8,128)S(1)}, f32[96,1024]{1,0:T(8,128)S(1)}, u32[]{:S(2)}, u32[]{:S(2)}) collective-permute-start(f32[96,1024]{1,0:T(8,128)S(1)} %get-tuple-element.44), channel_id=1, source_target_pairs={{0,1},{1,0},{2,3},{3,2},{4,5},{5,4},{6,7},{7,6},{8,9},{9,8},{10,11... | collective-permute-start | bytes 1179656 | tf_op jit(solution)/shard_map/ppermute | solution.py:218
  43.7 10.1 %collective-permute-start.4 = (f32[96,1024]{1,0:T(8,128)S(1)}, f32[96,1024]{1,0:T(8,128)S(1)}, u32[]{:S(2)}, u32[]{:S(2)}) collective-permute-start(f32[96,1024]{1,0:T(8,128)S(1)} %get-tuple-element.36), channel_id=1, source_target_pairs={{0,1},{1,0},{2,3},{3,2},{4,5},{5,4},{6,7},{7,6},{8,9},{9,8},{10,11... | collective-permute-start | bytes 1179656 | tf_op jit(solution)/shard_map/ppermute | solution.py:218
  47.0 8.5 %collective-permute-start.10 = (f32[96,1024]{1,0:T(8,128)S(1)}, f32[96,1024]{1,0:T(8,128)S(1)}, u32[]{:S(2)}, u32[]{:S(2)}) collective-permute-start(f32[96,1024]{1,0:T(8,128)S(1)} %get-tuple-element.42), channel_id=1, source_target_pairs={{0,1},{1,0},{2,3},{3,2},{4,5},{5,4},{6,7},{7,6},{8,9},{9,8},{10,11... | collective-permute-start | bytes 1179656 | tf_op jit(solution)/shard_map/ppermute | solution.py:219
  47.7 11.8 %collective-permute-start.12 = (f32[96,1024]{1,0:T(8,128)S(1)}, f32[96,1024]{1,0:T(8,128)S(1)}, u32[]{:S(2)}, u32[]{:S(2)}) collective-permute-start(f32[96,1024]{1,0:T(8,128)S(1)} %add.56), channel_id=1, source_target_pairs={{0,2},{1,5},{2,0},{3,7},{4,6},{5,1},{6,4},{7,3},{8,10},{9,13},{10,... | collective-permute-start | bytes 1179656 | tf_op jit(solution)/shard_map/ppermute | solution.py:220
  53.0 10.0 %collective-permute-start.3 = (f32[96,1024]{1,0:T(8,128)S(1)}, f32[96,1024]{1,0:T(8,128)S(1)}, u32[]{:S(2)}, u32[]{:S(2)}) collective-permute-start(f32[96,1024]{1,0:T(8,128)S(1)} %get-tuple-element.34), channel_id=1, source_target_pairs={{0,1},{1,0},{2,3},{3,2},{4,5},{5,4},{6,7},{7,6},{8,9},{9,8},{10,11... | collective-permute-start | bytes 1179656 | tf_op jit(solution)/shard_map/ppermute | solution.py:219
  53.9 18.5 %collective-permute-start.5 = (f32[96,1024]{1,0:T(8,128)S(1)}, f32[96,1024]{1,0:T(8,128)S(1)}, u32[]{:S(2)}, u32[]{:S(2)}) collective-permute-start(f32[96,1024]{1,0:T(8,128)S(1)} %add.50), channel_id=1, source_target_pairs={{0,2},{1,5},{2,0},{3,7},{4,6},{5,1},{6,4},{7,3},{8,10},{9,13},{10,... | collective-permute-start | bytes 1179656 | tf_op jit(solution)/shard_map/ppermute | solution.py:220
  59.5 14.9 %collective-permute-start.13 = (f32[96,512]{1,0:T(8,128)S(1)}, f32[96,512]{1,0:T(8,128)S(1)}, u32[]{:S(2)}, u32[]{:S(2)}) collective-permute-start(f32[96,512]{1,0:T(8,128)S(1)} %slice.19), channel_id=1, source_target_pairs={{0,4},{1,3},{2,6},{3,1},{4,0},{5,7},{6,2},{7,5},{8,12},{9,11},{10,... | collective-permute-start | bytes 589832 | tf_op jit(solution)/shard_map/ppermute | solution.py:222
  72.5 7.6 %collective-permute-start.6 = (f32[96,512]{1,0:T(8,128)S(1)}, f32[96,512]{1,0:T(8,128)S(1)}, u32[]{:S(2)}, u32[]{:S(2)}) collective-permute-start(f32[96,512]{1,0:T(8,128)S(1)} %slice.17), channel_id=1, source_target_pairs={{0,4},{1,3},{2,6},{3,1},{4,0},{5,7},{6,2},{7,5},{8,12},{9,11},{10,... | collective-permute-start | bytes 589832 | tf_op jit(solution)/shard_map/ppermute | solution.py:222

commit v2 on v1

--- a/solution.py
+++ b/solution.py
@@ -14,6 +14,7 @@
 VMEM = pl.BlockSpec(memory_space=pltpu.VMEM)
 SMEM = pl.BlockSpec(memory_space=pltpu.SMEM)
 HBM = pl.BlockSpec(memory_space=pltpu.HBM)
+ANY = pl.BlockSpec(memory_space=pl.ANY)
 F32 = jnp.float32
 LIGHT = pl.CostEstimate(flops=1, bytes_accessed=1, transcendentals=0)
 
@@ -131,7 +132,7 @@
     width = dosage.shape[1] // 2
     return pl.pallas_call(
         functools.partial(loads_kernel, False),
-        in_specs=[SMEM, VMEM, HBM, VMEM, VMEM, VMEM],
+        in_specs=[SMEM, VMEM, HBM] + [VMEM] * 3,
         out_specs=[VMEM] * (len(CHUNKS) + 1),
         out_shape=[jax.ShapeDtypeStruct((many, width), F32) for many in CHUNKS]
         + [pltpu.VMEM((2, rows, width), jnp.bfloat16)],
@@ -143,9 +144,34 @@
     )(place, probe_b, *in_hbm(dosage), mean, sums, *in_vmem(held))
 
 
-def apply_kernel(first, factor, shrink, place, *refs):
-    if first:
-        own, other, mean, scale, held, sent, kept, left_out, shift_out = refs
+def add_kernel(count, order, *refs):
+    values, outs = refs[:count], refs[count + order :]
+    total = values[0][...]
+    for value in values[1:]:
+        total = total + value[...]
+    width = outs[0].shape[1]
+    for index, out in enumerate(outs):
+        out[...] = total[:, index * width : (index + 1) * width]
+
+
+def add_up(*arrays, after=(), cut=1):
+    many, width = arrays[0].shape
+    count = len(arrays)
+    return pl.pallas_call(
+        functools.partial(add_kernel, count, len(after)),
+        in_specs=[VMEM] * count + [ANY] * len(after),
+        out_specs=[VMEM] * cut,
+        out_shape=[jax.ShapeDtypeStruct((many, width // cut), F32)] * cut,
+        compiler_params=pltpu.CompilerParams(vmem_limit_bytes=LIMIT),
+        cost_estimate=LIGHT,
+        name="add_up",
+    )(*arrays, *after)
+
+
+def apply_kernel(first, swapped, factor, shrink, place, *refs):
+    if first:
+        own, other, mean, scale, held = refs[:5]
+        sent, kept, left_out, shift_out = refs[-4:]
         half = place[0]
         width = own.shape[1]
         lefts, shift = [], 0.0
@@ -159,12 +185,13 @@
         shift = shift * shrink
         shift_out[...] = jnp.broadcast_to(shift, shift_out.shape)
     else:
-        left_in, shift_in, held, sent, kept = refs
+        left_in, shift_in, held = refs[:3]
+        sent, kept = refs[-2:]
         lefts = [left_in[0], left_in[1]]
         shift = shift_in[:, :1]
     core, z = place[1], place[2]
     block = held.shape[1] // 8
-    mask = 1 + core
+    mask = 2 - core if swapped else 1 + core
     for out, one, two, owner in ((sent, mask, 3 - mask, 1 - core), (kept, 3 - mask, mask, core)):
         for index, flip in enumerate((two, 3) if first else (0, one)):
             at = pl.ds(pl.multiple_of(((z ^ flip) * 2 + owner) * block, block), block)
@@ -176,7 +203,7 @@
             out[:, index * block : (index + 1) * block] = product * shrink - shift
 
 
-def apply_rows(first, factor, shrink, place, *arrays):
+def apply_rows(first, factor, shrink, place, *arrays, after, swapped=False):
     many = arrays[0].shape[-2]
     held = arrays[-1]
     wide = held.shape[1] // 4
@@ -187,14 +214,14 @@
             jax.ShapeDtypeStruct((many, 128), F32),
         ]
     return pl.pallas_call(
-        functools.partial(apply_kernel, first, factor, shrink),
-        in_specs=[SMEM] + [VMEM] * len(arrays),
+        functools.partial(apply_kernel, first, swapped, factor, shrink),
+        in_specs=[SMEM] + [VMEM] * len(arrays) + [ANY] * len(after),
         out_specs=[VMEM] * len(out_shape),
         out_shape=out_shape,
         compiler_params=pltpu.CompilerParams(vmem_limit_bytes=LIMIT),
         cost_estimate=LIGHT,
         name="apply_first" if first else "apply_second",
-    )(place, *arrays[:-1], *in_vmem(held))
+    )(place, *arrays[:-1], *in_vmem(held), *after)
 
 
 def on_slice(dosage, allele_mean, allele_scale, probes):
@@ -205,22 +232,40 @@
     half = jnp.where(core == 0, sample % 2, sample // 2)
     place = jnp.stack([half, core, z]).astype(jnp.int32)
     mean, scale = allele_mean[None, :], allele_scale[None, :]
-    *sent, probe_b, sums, held = first_half(place, probes, dosage, mean)
-    *kept, held = second_half(place, probe_b, dosage, mean, sums, held)
     factor, shrink = total**-0.5, across**-0.5
-    results = []
-    for part, own in zip(sent, kept):
-        own = own + lax.ppermute(part, AXES, PLANE_FIRST)
-        own = own + lax.ppermute(own, AXES, PLANE_SECOND)
-        other = lax.ppermute(own, AXES, PLANE_FIRST)
-        sent_a, kept_a, left, shift = apply_rows(True, factor, shrink, place, own, other, mean, scale, held)
-        sent_b, kept_b = apply_rows(False, factor, shrink, place, left, shift, held)
-        kept_a = kept_a + lax.ppermute(sent_a, AXES, CORES)
-        kept_b = kept_b + lax.ppermute(sent_b, AXES, CORES)
-        kept_b = kept_b + lax.ppermute(kept_a, AXES, LINE_FIRST)
-        width = kept_b.shape[1] // 2
-        results.append(kept_b[:, :width] + lax.ppermute(kept_b[:, width:], AXES, LINE_SECOND))
-    return jnp.concatenate(results, axis=0)
+    send = lambda array, moves: lax.ppermute(array, AXES, moves)
+
+    apply_first = functools.partial(apply_rows, True, factor, shrink, place)
+    apply_second = functools.partial(apply_rows, False, factor, shrink, place)
+
+    sent_a, sent_b, probe_b, sums, held = first_half(place, probes, dosage, mean)
+    got_a, got_b = send(sent_a, PLANE_FIRST), send(sent_b, PLANE_FIRST)
+    own_a, own_b, held = second_half(place, probe_b, dosage, mean, sums, held)
+    (own_a,) = add_up(own_a, got_a)
+    got_a = send(own_a, PLANE_SECOND)
+    (own_b,) = add_up(own_b, got_b, after=[own_a])
+    got_b = send(own_b, PLANE_SECOND)
+    (own_a,) = add_up(own_a, got_a, after=[own_b])
+    other_a = send(own_a, PLANE_FIRST)
+    (own_b,) = add_up(own_b, got_b, after=[own_a])
+    other_b = send(own_b, PLANE_FIRST)
+    sent, far_a, left, shift = apply_first(own_a, other_a, mean, scale, held, after=[own_b])
+    (far_a,) = add_up(far_a, send(sent, CORES))
+    got_a = send(far_a, LINE_FIRST)
+    sent, near_a = apply_second(left, shift, held, after=[far_a])
+    core_a = send(sent, CORES)
+    sent, far_b, left, shift = apply_first(own_b, other_b, mean, scale, held, after=[near_a], swapped=True)
+    core_b = send(sent, CORES)
+    (near_a,) = add_up(near_a, got_a, after=[far_b])
+    near_a, sent_a = add_up(near_a, core_a, cut=2)
+    (far_b,) = add_up(far_b, core_b, after=[near_a])
+    got_a, got_b = send(sent_a, LINE_SECOND), send(far_b, LINE_SECOND)
+    sent, near_b = apply_second(left, shift, held, after=[far_b], swapped=True)
+    core_b = send(sent, CORES)
+    (near_b,) = add_up(near_b, got_b)
+    near_b, sent_b = add_up(near_b, core_b, cut=2)
+    got_b = send(sent_b, LINE_FIRST)
+    return jnp.concatenate([near_a + got_a, near_b + got_b], axis=0)
 
 
 def on_any(dosage, allele_mean, allele_scale, probes):

time: 81.2 us -> 72.8 us (0.90)
  waiting for transfers between devices: 33.9 us -> 26.6 us
  starting transfers between devices: 22.3 us -> 20.5 us
    ppermute x14, waiting for transfers between devices: 33.9 us -> 26.6 us  [on_slice(): send = lambda array, moves: lax.ppermute(array, AXES, moves)]
    ppermute x14, starting transfers between devices: 22.3 us -> 20.5 us  [on_slice(): send = lambda array, moves: lax.ppermute(array, AXES, moves)]
    pallas_call x4 -> x14, Pallas kernels: 12.9 us -> 13.4 us  [the longest x4 13 us: apply_rows(): pl.pallas_call(functools.partial(apply_kernel, first, swapped, factor, sh...]
  transfers between devices with their start and end apart: 14 -> 14, of which waited for: 7 -> 6; matrix products, arithmetic and copies ran while one was open for 1% -> 0% of each run, Pallas kernels for 22% -> 21%
where the time goes in v2:
time: 72.8 us; the launch traced here: 71.9 us
  waiting for transfers between devices  26.6 us (37%)
  Pallas kernels  23.8 us (33%)
  starting transfers between devices  20.5 us (28%)
  other arithmetic  0.91 us (1%)
    ppermute x14, waiting for transfers between devices, on_slice(): send = lambda array, moves: lax.ppermute(array, AXES, moves)  26.6 us
    ppermute x14, starting transfers between devices, on_slice(): send = lambda array, moves: lax.ppermute(array, AXES, moves)  20.5 us
    pallas_call x4, Pallas kernels, apply_rows(): pl.pallas_call(functools.partial(apply_kernel, first, swapped, factor, sh...  13 us
    pallas_call x1, Pallas kernels, first_half(): pl.pallas_call(functools.partial(loads_kernel, True), in_specs=[SMEM, HBM...  5.5 us
    pallas_call x1, Pallas kernels, second_half(): pl.pallas_call(functools.partial(loads_kernel, False), in_specs=[SMEM, VM...  4.87 us
  transfers between devices with their start and end apart: 14, of which 6 were waited for; matrix products, arithmetic and copies ran while one was open for 0% of the time, Pallas kernels for 21%

profile of v2, /device:TPU:0, one launch (start us, length us, event | category | flops | bytes accessed | tf_op | source)
XLA Modules:
  0.0 71.9 jit_solution(11985977055557867281)
XLA Ops:
  0.0 0.1 pad_add_fusion.place
  0.1 5.5 %loads_sent.1 = (f32[96,1024]{1,0:T(8,128)S(1)}, f32[96,1024]{1,0:T(8,128)S(1)}, bf16[192,4096]{1,0:T(8,128)(2,1)S(1)}, f32[192,128]{1,0:T(8,128)S(1)}, bf16[2,4096,1024]{2,1,0:T(8,128)(2,1)S(1)}) custom-call(s32[3]{0:T(128)S(1)} %pad_add_fusion.place, f32[192,4096]{1,0:T(8,128)} %probes.1, bf16[4096,2048]{1,0:T(8,128)(2,1)} %dosage.3, f32[1,2048]{1,0:T(1,128)} %bitcast.5), custom_call_target="tpu_custom_call" | custom-call | flops 1 | bytes 1 | tf_op jit(solution)/shard_map/loads_sent/pallas_call | solution.py:107
  5.6 3.0 %collective-permute-start = (f32[96,1024]{1,0:T(8,128)S(1)}, f32[96,1024]{1,0:T(8,128)S(1)}, u32[]{:S(2)}, u32[]{:S(2)}) collective-permute-start(f32[96,1024]{1,0:T(8,128)S(1)} %get-tuple-element.33), channel_id=1, source_target_pairs={{0,8},{1,17},{2,10},{3,19},{4,12},{5,21},{6,14},{7,23},{8,0},{9,25... | collective-permute-start | bytes 1179656 | tf_op jit(solution)/shard_map/ppermute | solution.py:236
  8.6 0.1 collective-permute-start.2
  8.7 4.9 %loads_kept.1 = (f32[96,1024]{1,0:T(8,128)S(1)}, f32[96,1024]{1,0:T(8,128)S(1)}, bf16[2,4096,1024]{2,1,0:T(8,128)(2,1)S(1)}) custom-call(s32[3]{0:T(128)S(1)} %pad_add_fusion.place, bf16[192,4096]{1,0:T(8,128)(2,1)S(1)} %get-tuple-element.29.probes, bf16[4096,2048]{1,0:T(8,128)(2,1)} %dosage.3, ...), custom_call_target="tpu_custom_call", output_to_operand_aliasing={{2}: (5, {})} | custom-call | flops 1 | bytes 1 | tf_op jit(solution)/shard_map/loads_kept/pallas_call | solution.py:133
  13.6 0.8 %collective-permute-done.refs_1_ = f32[96,1024]{1,0:T(8,128)S(1)} collective-permute-done((f32[96,1024]{1,0:T(8,128)S(1)}, f32[96,1024]{1,0:T(8,128)S(1)}, u32[]{:S(2)}, u32[]{:S(2)}) %collective-permute-start) | collective-permute-done | bytes 393248 | tf_op jit(solution)/shard_map/ppermute | solution.py:236
  14.4 2.1 %collective-permute-start.1 = (f32[96,1024]{1,0:T(8,128)S(1)}, f32[96,1024]{1,0:T(8,128)S(1)}, u32[]{:S(2)}, u32[]{:S(2)}) collective-permute-start(f32[96,1024]{1,0:T(8,128)S(1)} %add_up.10.refs_2_.refs_0_), channel_id=1, source_target_pairs={{0,16},{1,9},{2,18},{3,11},{4,20},{5,13},{6,22},{7,15},{8,24},{9,1... | collective-permute-start | bytes 1179656 | tf_op jit(solution)/shard_map/ppermute | solution.py:236
  16.5 4.2 %collective-permute-done.2.refs_1_ = f32[96,1024]{1,0:T(8,128)S(1)} collective-permute-done((f32[96,1024]{1,0:T(8,128)S(1)}, f32[96,1024]{1,0:T(8,128)S(1)}, u32[]{:S(2)}, u32[]{:S(2)}) %collective-permute-start.2) | collective-permute-done | bytes 393248 | tf_op jit(solution)/shard_map/ppermute | solution.py:236
  20.8 2.4 %collective-permute-start.4 = (f32[96,1024]{1,0:T(8,128)S(1)}, f32[96,1024]{1,0:T(8,128)S(1)}, u32[]{:S(2)}, u32[]{:S(2)}) collective-permute-start(f32[96,1024]{1,0:T(8,128)S(1)} %add_up.11.refs_2_.refs_0_), channel_id=1, source_target_pairs={{0,16},{1,9},{2,18},{3,11},{4,20},{5,13},{6,22},{7,15},{8,24},{9,1... | collective-permute-start | bytes 1179656 | tf_op jit(solution)/shard_map/ppermute | solution.py:236
  23.2 0.0 collective-permute-done.1.refs_1_
  23.2 1.6 %collective-permute-start.3 = (f32[96,1024]{1,0:T(8,128)S(1)}, f32[96,1024]{1,0:T(8,128)S(1)}, u32[]{:S(2)}, u32[]{:S(2)}) collective-permute-start(f32[96,1024]{1,0:T(8,128)S(1)} %add_up.12.refs_2_.refs_0_), channel_id=1, source_target_pairs={{0,8},{1,17},{2,10},{3,19},{4,12},{5,21},{6,14},{7,23},{8,0},{9,25... | collective-permute-start | bytes 1179656 | tf_op jit(solution)/shard_map/ppermute | solution.py:236
  24.8 7.5 %collective-permute-done.4.refs_1_ = f32[96,1024]{1,0:T(8,128)S(1)} collective-permute-done((f32[96,1024]{1,0:T(8,128)S(1)}, f32[96,1024]{1,0:T(8,128)S(1)}, u32[]{:S(2)}, u32[]{:S(2)}) %collective-permute-start.4) | collective-permute-done | bytes 393248 | tf_op jit(solution)/shard_map/ppermute | solution.py:236
  32.3 0.0 collective-permute-done.3.refs_1_
  32.3 3.3 %apply_first.2 = (f32[96,1024]{1,0:T(8,128)S(1)}, f32[96,1024]{1,0:T(8,128)S(1)}, bf16[2,96,1024]{2,1,0:T(8,128)(2,1)S(1)}, f32[96,128]{1,0:T(8,128)S(1)}) custom-call(s32[3]{0:T(128)S(1)} %pad_add_fusion.place, f32[96,1024]{1,0:T(8,128)S(1)} %add_up.12.refs_2_.refs_0_, f32[96,1024]{1,0:T(8,128)S(1)} %collective-permute-done.3.refs_1_, ...), custom_call_target="tpu_custom_call" | custom-call | flops 1 | bytes 1 | tf_op jit(solution)/shard_map/apply_first/pallas_call | solution.py:216
  35.6 0.7 collective-permute-start.5
  36.3 2.0 %collective-permute-start.7 = (f32[96,1024]{1,0:T(8,128)S(1)}, f32[96,1024]{1,0:T(8,128)S(1)}, u32[]{:S(2)}, u32[]{:S(2)}) collective-permute-start(f32[96,1024]{1,0:T(8,128)S(1)} %add_up.13.refs_5_.refs_0_), channel_id=1, source_target_pairs={{0,8},{1,17},{2,10},{3,19},{4,12},{5,21},{6,14},{7,23},{8,0},{9,25... | collective-permute-start | bytes 1179656 | tf_op jit(solution)/shard_map/ppermute | solution.py:236
  38.3 0.0 collective-permute-done.5.refs_1_
  38.3 1.6 %collective-permute-start.6 = (f32[96,1024]{1,0:T(8,128)S(1)}, f32[96,1024]{1,0:T(8,128)S(1)}, u32[]{:S(2)}, u32[]{:S(2)}) collective-permute-start(f32[96,1024]{1,0:T(8,128)S(1)} %add_up.14.refs_3_), channel_id=1, source_target_pairs={{0,2},{1,5},{2,0},{3,7},{4,6},{5,1},{6,4},{7,3},{8,10},{9,13},{10,... | collective-permute-start | bytes 1179656 | tf_op jit(solution)/shard_map/ppermute | solution.py:236
  40.0 3.2 %apply_second.2 = (f32[96,1024]{1,0:T(8,128)S(1)}, f32[96,1024]{1,0:T(8,128)S(1)}) custom-call(s32[3]{0:T(128)S(1)} %pad_add_fusion.place, bf16[2,96,1024]{2,1,0:T(8,128)(2,1)S(1)} %get-tuple-element.37.refs_0_, f32[96,128]{1,0:T(8,128)S(1)} %get-tuple-element.38.refs_1_, bf16[2,4096,1024]{2,1,0:T(8,128)(2,1)S(1)} %get-tuple-element.36.refs_4_.refs_2_, ...), custom_call_target="tpu_custom_call" | custom-call | flops 1 | bytes 1 | tf_op jit(solution)/shard_map/apply_second/pallas_call | solution.py:216
  43.2 1.0 %collective-permute-start.8 = (f32[96,1024]{1,0:T(8,128)S(1)}, f32[96,1024]{1,0:T(8,128)S(1)}, u32[]{:S(2)}, u32[]{:S(2)}) collective-permute-start(f32[96,1024]{1,0:T(8,128)S(1)} %get-tuple-element.43), channel_id=1, source_target_pairs={{0,1},{1,0},{2,3},{3,2},{4,5},{5,4},{6,7},{7,6},{8,9},{9,8},{10,11... | collective-permute-start | bytes 1179656 | tf_op jit(solution)/shard_map/ppermute | solution.py:236
  44.2 3.2 %apply_first.3 = (f32[96,1024]{1,0:T(8,128)S(1)}, f32[96,1024]{1,0:T(8,128)S(1)}, bf16[2,96,1024]{2,1,0:T(8,128)(2,1)S(1)}, f32[96,128]{1,0:T(8,128)S(1)}) custom-call(s32[3]{0:T(128)S(1)} %pad_add_fusion.place, f32[96,1024]{1,0:T(8,128)S(1)} %add_up.13.refs_5_.refs_0_, f32[96,1024]{1,0:T(8,128)S(1)} %collective-permute-done.7.refs_1_, ...), custom_call_target="tpu_custom_call" | custom-call | flops 1 | bytes 1 | tf_op jit(solution)/shard_map/apply_first/pallas_call | solution.py:216
  47.5 0.1 collective-permute-start.10
  47.6 2.8 %collective-permute-done.6.refs_1_ = f32[96,1024]{1,0:T(8,128)S(1)} collective-permute-done((f32[96,1024]{1,0:T(8,128)S(1)}, f32[96,1024]{1,0:T(8,128)S(1)}, u32[]{:S(2)}, u32[]{:S(2)}) %collective-permute-start.6) | collective-permute-done | bytes 393248 | tf_op jit(solution)/shard_map/ppermute | solution.py:236
  50.6 1.8 %collective-permute-start.11 = (f32[96,1024]{1,0:T(8,128)S(1)}, f32[96,1024]{1,0:T(8,128)S(1)}, u32[]{:S(2)}, u32[]{:S(2)}) collective-permute-start(f32[96,1024]{1,0:T(8,128)S(1)} %add_up.17.refs_3_), channel_id=1, source_target_pairs={{0,4},{1,3},{2,6},{3,1},{4,0},{5,7},{6,2},{7,5},{8,12},{9,11},{10,... | collective-permute-start | bytes 1179656 | tf_op jit(solution)/shard_map/ppermute | solution.py:236
  52.4 3.2 %apply_second.3 = (f32[96,1024]{1,0:T(8,128)S(1)}, f32[96,1024]{1,0:T(8,128)S(1)}) custom-call(s32[3]{0:T(128)S(1)} %pad_add_fusion.place, bf16[2,96,1024]{2,1,0:T(8,128)(2,1)S(1)} %get-tuple-element.46.refs_0_, f32[96,128]{1,0:T(8,128)S(1)} %get-tuple-element.47.refs_1_, bf16[2,4096,1024]{2,1,0:T(8,128)(2,1)S(1)} %get-tuple-element.36.refs_4_.refs_2_, ...), custom_call_target="tpu_custom_call" | custom-call | flops 1 | bytes 1 | tf_op jit(solution)/shard_map/apply_second/pallas_call | solution.py:216
  55.6 0.1 collective-permute-start.12
  55.7 2.1 %collective-permute-start.9 = (f32[96,512]{1,0:T(8,128)S(1)}, f32[96,512]{1,0:T(8,128)S(1)}, u32[]{:S(2)}, u32[]{:S(2)}) collective-permute-start(f32[96,512]{1,0:T(8,128)S(1)} %get-tuple-element.45), channel_id=1, source_target_pairs={{0,4},{1,3},{2,6},{3,1},{4,0},{5,7},{6,2},{7,5},{8,12},{9,11},{10,... | collective-permute-start | bytes 589832 | tf_op jit(solution)/shard_map/ppermute | solution.py:236
  57.7 5.1 %collective-permute-done.11.refs_1_ = f32[96,1024]{1,0:T(8,128)S(1)} collective-permute-done((f32[96,1024]{1,0:T(8,128)S(1)}, f32[96,1024]{1,0:T(8,128)S(1)}, u32[]{:S(2)}, u32[]{:S(2)}) %collective-permute-start.11) | collective-permute-done | bytes 393248 | tf_op jit(solution)/shard_map/ppermute | solution.py:236
  62.9 0.1 add_up.19
  62.9 2.0 %collective-permute-start.13 = (f32[96,512]{1,0:T(8,128)S(1)}, f32[96,512]{1,0:T(8,128)S(1)}, u32[]{:S(2)}, u32[]{:S(2)}) collective-permute-start(f32[96,512]{1,0:T(8,128)S(1)} %get-tuple-element.52), channel_id=1, source_target_pairs={{0,2},{1,5},{2,0},{3,7},{4,6},{5,1},{6,4},{7,3},{8,10},{9,13},{10,... | collective-permute-start | bytes 589832 | tf_op jit(solution)/shard_map/ppermute | solution.py:236
  65.0 6.1 %collective-permute-done.9 = f32[96,512]{1,0:T(8,128)S(1)} collective-permute-done((f32[96,512]{1,0:T(8,128)S(1)}, f32[96,512]{1,0:T(8,128)S(1)}, u32[]{:S(2)}, u32[]{:S(2)}) %collective-permute-start.9) | collective-permute-done | bytes 196640 | tf_op jit(solution)/shard_map/ppermute | solution.py:236
  71.2 0.8 %pad_maximum_fusion = f32[192,512]{1,0:T(8,128)} fusion(f32[96,512]{1,0:T(8,128)S(1)} %add.18, f32[96,512]{1,0:T(8,128)S(1)} %add.17), kind=kLoop, calls=%fused_computation | loop fusion | flops 98304 | bytes 786432 | tf_op jit(solution)/shard_map/concatenate | solution.py:268
  (20 shorter events, 0.5 us)
Async XLA Ops:
  0.0 8.7 %copy-start = (f32[2048]{0:T(1024)S(1)}, f32[2048]{0:T(1024)}, u32[]{:S(2)}) copy-start(f32[2048]{0:T(1024)} %param.5) | copy-start | bytes 24580
  5.6 8.8 %collective-permute-start = (f32[96,1024]{1,0:T(8,128)S(1)}, f32[96,1024]{1,0:T(8,128)S(1)}, u32[]{:S(2)}, u32[]{:S(2)}) collective-permute-start(f32[96,1024]{1,0:T(8,128)S(1)} %get-tuple-element.33), channel_id=1, source_target_pairs={{0,8},{1,17},{2,10},{3,19},{4,12},{5,21},{6,14},{7,23},{8,0},{9,25... | collective-permute-start | bytes 1179656 | tf_op jit(solution)/shard_map/ppermute | solution.py:236
  8.6 12.1 %collective-permute-start.2 = (f32[96,1024]{1,0:T(8,128)S(1)}, f32[96,1024]{1,0:T(8,128)S(1)}, u32[]{:S(2)}, u32[]{:S(2)}) collective-permute-start(f32[96,1024]{1,0:T(8,128)S(1)} %get-tuple-element.35), channel_id=1, source_target_pairs={{0,8},{1,17},{2,10},{3,19},{4,12},{5,21},{6,14},{7,23},{8,0},{9,25... | collective-permute-start | bytes 1179656 | tf_op jit(solution)/shard_map/ppermute | solution.py:236
  8.7 23.7 %copy-start.1 = (f32[2048]{0:T(1024)S(1)}, f32[2048]{0:T(1024)}, u32[]{:S(2)}) copy-start(f32[2048]{0:T(1024)} %param.6) | copy-start | bytes 24580
  14.4 8.8 %collective-permute-start.1 = (f32[96,1024]{1,0:T(8,128)S(1)}, f32[96,1024]{1,0:T(8,128)S(1)}, u32[]{:S(2)}, u32[]{:S(2)}) collective-permute-start(f32[96,1024]{1,0:T(8,128)S(1)} %add_up.10.refs_2_.refs_0_), channel_id=1, source_target_pairs={{0,16},{1,9},{2,18},{3,11},{4,20},{5,13},{6,22},{7,15},{8,24},{9,1... | collective-permute-start | bytes 1179656 | tf_op jit(solution)/shard_map/ppermute | solution.py:236
  20.8 11.5 %collective-permute-start.4 = (f32[96,1024]{1,0:T(8,128)S(1)}, f32[96,1024]{1,0:T(8,128)S(1)}, u32[]{:S(2)}, u32[]{:S(2)}) collective-permute-start(f32[96,1024]{1,0:T(8,128)S(1)} %add_up.11.refs_2_.refs_0_), channel_id=1, source_target_pairs={{0,16},{1,9},{2,18},{3,11},{4,20},{5,13},{6,22},{7,15},{8,24},{9,1... | collective-permute-start | bytes 1179656 | tf_op jit(solution)/shard_map/ppermute | solution.py:236
  23.2 9.1 %collective-permute-start.3 = (f32[96,1024]{1,0:T(8,128)S(1)}, f32[96,1024]{1,0:T(8,128)S(1)}, u32[]{:S(2)}, u32[]{:S(2)}) collective-permute-start(f32[96,1024]{1,0:T(8,128)S(1)} %add_up.12.refs_2_.refs_0_), channel_id=1, source_target_pairs={{0,8},{1,17},{2,10},{3,19},{4,12},{5,21},{6,14},{7,23},{8,0},{9,25... | collective-permute-start | bytes 1179656 | tf_op jit(solution)/shard_map/ppermute | solution.py:236
  35.6 2.7 %collective-permute-start.5 = (f32[96,1024]{1,0:T(8,128)S(1)}, f32[96,1024]{1,0:T(8,128)S(1)}, u32[]{:S(2)}, u32[]{:S(2)}) collective-permute-start(f32[96,1024]{1,0:T(8,128)S(1)} %get-tuple-element.40), channel_id=1, source_target_pairs={{0,1},{1,0},{2,3},{3,2},{4,5},{5,4},{6,7},{7,6},{8,9},{9,8},{10,11... | collective-permute-start | bytes 1179656 | tf_op jit(solution)/shard_map/ppermute | solution.py:236
  36.3 7.9 %collective-permute-start.7 = (f32[96,1024]{1,0:T(8,128)S(1)}, f32[96,1024]{1,0:T(8,128)S(1)}, u32[]{:S(2)}, u32[]{:S(2)}) collective-permute-start(f32[96,1024]{1,0:T(8,128)S(1)} %add_up.13.refs_5_.refs_0_), channel_id=1, source_target_pairs={{0,8},{1,17},{2,10},{3,19},{4,12},{5,21},{6,14},{7,23},{8,0},{9,25... | collective-permute-start | bytes 1179656 | tf_op jit(solution)/shard_map/ppermute | solution.py:236
  38.3 12.1 %collective-permute-start.6 = (f32[96,1024]{1,0:T(8,128)S(1)}, f32[96,1024]{1,0:T(8,128)S(1)}, u32[]{:S(2)}, u32[]{:S(2)}) collective-permute-start(f32[96,1024]{1,0:T(8,128)S(1)} %add_up.14.refs_3_), channel_id=1, source_target_pairs={{0,2},{1,5},{2,0},{3,7},{4,6},{5,1},{6,4},{7,3},{8,10},{9,13},{10,... | collective-permute-start | bytes 1179656 | tf_op jit(solution)/shard_map/ppermute | solution.py:236
  43.2 7.2 %collective-permute-start.8 = (f32[96,1024]{1,0:T(8,128)S(1)}, f32[96,1024]{1,0:T(8,128)S(1)}, u32[]{:S(2)}, u32[]{:S(2)}) collective-permute-start(f32[96,1024]{1,0:T(8,128)S(1)} %get-tuple-element.43), channel_id=1, source_target_pairs={{0,1},{1,0},{2,3},{3,2},{4,5},{5,4},{6,7},{7,6},{8,9},{9,8},{10,11... | collective-permute-start | bytes 1179656 | tf_op jit(solution)/shard_map/ppermute | solution.py:236
  47.5 3.0 %collective-permute-start.10 = (f32[96,1024]{1,0:T(8,128)S(1)}, f32[96,1024]{1,0:T(8,128)S(1)}, u32[]{:S(2)}, u32[]{:S(2)}) collective-permute-start(f32[96,1024]{1,0:T(8,128)S(1)} %get-tuple-element.48), channel_id=1, source_target_pairs={{0,1},{1,0},{2,3},{3,2},{4,5},{5,4},{6,7},{7,6},{8,9},{9,8},{10,11... | collective-permute-start | bytes 1179656 | tf_op jit(solution)/shard_map/ppermute | solution.py:236
  50.6 12.3 %collective-permute-start.11 = (f32[96,1024]{1,0:T(8,128)S(1)}, f32[96,1024]{1,0:T(8,128)S(1)}, u32[]{:S(2)}, u32[]{:S(2)}) collective-permute-start(f32[96,1024]{1,0:T(8,128)S(1)} %add_up.17.refs_3_), channel_id=1, source_target_pairs={{0,4},{1,3},{2,6},{3,1},{4,0},{5,7},{6,2},{7,5},{8,12},{9,11},{10,... | collective-permute-start | bytes 1179656 | tf_op jit(solution)/shard_map/ppermute | solution.py:236
  55.6 7.3 %collective-permute-start.12 = (f32[96,1024]{1,0:T(8,128)S(1)}, f32[96,1024]{1,0:T(8,128)S(1)}, u32[]{:S(2)}, u32[]{:S(2)}) collective-permute-start(f32[96,1024]{1,0:T(8,128)S(1)} %get-tuple-element.50), channel_id=1, source_target_pairs={{0,1},{1,0},{2,3},{3,2},{4,5},{5,4},{6,7},{7,6},{8,9},{9,8},{10,11... | collective-permute-start | bytes 1179656 | tf_op jit(solution)/shard_map/ppermute | solution.py:236
  55.7 15.4 %collective-permute-start.9 = (f32[96,512]{1,0:T(8,128)S(1)}, f32[96,512]{1,0:T(8,128)S(1)}, u32[]{:S(2)}, u32[]{:S(2)}) collective-permute-start(f32[96,512]{1,0:T(8,128)S(1)} %get-tuple-element.45), channel_id=1, source_target_pairs={{0,4},{1,3},{2,6},{3,1},{4,0},{5,7},{6,2},{7,5},{8,12},{9,11},{10,... | collective-permute-start | bytes 589832 | tf_op jit(solution)/shard_map/ppermute | solution.py:236
  62.9 8.2 %collective-permute-start.13 = (f32[96,512]{1,0:T(8,128)S(1)}, f32[96,512]{1,0:T(8,128)S(1)}, u32[]{:S(2)}, u32[]{:S(2)}) collective-permute-start(f32[96,512]{1,0:T(8,128)S(1)} %get-tuple-element.52), channel_id=1, source_target_pairs={{0,2},{1,5},{2,0},{3,7},{4,6},{5,1},{6,4},{7,3},{8,10},{9,13},{10,... | collective-permute-start | bytes 589832 | tf_op jit(solution)/shard_map/ppermute | solution.py:236

commit v3 on v2

--- a/solution.py
+++ b/solution.py
@@ -10,6 +10,7 @@
 AXES = ("sample", "snp")
 CHUNKS = (96, 96)
 STEPS = 8
+PIECES = 2
 LIMIT = 20 * 1024 * 1024
 VMEM = pl.BlockSpec(memory_space=pltpu.VMEM)
 SMEM = pl.BlockSpec(memory_space=pltpu.SMEM)
@@ -146,10 +147,17 @@
 
 def add_kernel(count, order, *refs):
     values, outs = refs[:count], refs[count + order :]
-    total = values[0][...]
-    for value in values[1:]:
+    width = outs[0].shape[1]
+    whole, pieces = values[0], values[1:]
+    if pieces[0].shape[1] < whole.shape[1]:
+        narrow = pieces[0].shape[1]
+        for index, piece in enumerate(pieces):
+            low = index * narrow
+            outs[low // width][:, low % width : low % width + narrow] = whole[:, low : low + narrow] + piece[...]
+        return
+    total = whole[...]
+    for value in pieces:
         total = total + value[...]
-    width = outs[0].shape[1]
     for index, out in enumerate(outs):
         out[...] = total[:, index * width : (index + 1) * width]
 
@@ -168,60 +176,114 @@
     )(*arrays, *after)
 
 
-def apply_kernel(first, swapped, factor, shrink, place, *refs):
-    if first:
-        own, other, mean, scale, held = refs[:5]
-        sent, kept, left_out, shift_out = refs[-4:]
-        half = place[0]
-        width = own.shape[1]
-        lefts, shift = [], 0.0
-        for slot, ref, at in ((0, other, 1 - half), (1, own, half)):
-            span = pl.ds(pl.multiple_of(at * width, width), width)
-            gain = scale[:, span]
-            left = (ref[...] * (gain * gain * factor)).astype(jnp.bfloat16)
-            shift = shift + jnp.sum(left.astype(F32) * mean[:, span], axis=1, keepdims=True)
-            left_out[slot] = left
+def scaled(ref, gain, middle, factor):
+    left = (ref[...] * (gain * gain * factor)).astype(jnp.bfloat16)
+    return left, jnp.sum(left.astype(F32) * middle, axis=1, keepdims=True)
+
+
+def blocks(place, held, swapped):
+    core, z = place[1], place[2]
+    block = held.shape[1] // 8
+    mask = 2 - core if swapped else 1 + core
+    flips = [(3 - mask, 1 - core), (3, 1 - core), (mask, core), (3, core)]
+    flips += [(0, 1 - core), (mask, 1 - core), (0, core), (3 - mask, core)]
+    return [pl.ds(pl.multiple_of(((z ^ flip) * 2 + owner) * block, block), block) for flip, owner in flips]
+
+
+def times(left, held, slot, at):
+    return lax.dot_general(left, held[slot, at], (((1,), (1,)), ((), ())), preferred_element_type=F32)
+
+
+def half_span(half, width):
+    return pl.ds(pl.multiple_of(half * width, width), width)
+
+
+def own_kernel(swapped, factor, place, own, mean, scale, held, *refs):
+    partial, shift_out = refs[-2:]
+    span = half_span(place[0], own.shape[1])
+    left, shift = scaled(own, scale[:, span], mean[:, span], factor)
+    shift_out[...] = jnp.broadcast_to(shift, shift_out.shape)
+    block = held.shape[1] // 8
+    for index, at in enumerate(blocks(place, held, swapped)):
+        partial[:, index * block : (index + 1) * block] = times(left, held, 1, at)
+
+
+def apply_kernel(first, split, swapped, factor, shrink, place, *refs):
+    if first:
+        other, own, mean, scale, held = refs[:5]
+        *pieces, kept, left_out, shift_out = refs[-3 - PIECES :]
+        span = half_span(1 - place[0], other.shape[1])
+        left, shift = scaled(other, scale[:, span], mean[:, span], factor)
+        left_out[0] = left
+        lefts = [left]
+        if split:
+            partial, shift_own = own, refs[5][:, :1]
+        else:
+            span = half_span(place[0], own.shape[1])
+            left, shift_own = scaled(own, scale[:, span], mean[:, span], factor)
+            left_out[1] = left
             lefts.append(left)
-        shift = shift * shrink
+        shift = (shift + shift_own) * shrink
         shift_out[...] = jnp.broadcast_to(shift, shift_out.shape)
     else:
         left_in, shift_in, held = refs[:3]
-        sent, kept = refs[-2:]
-        lefts = [left_in[0], left_in[1]]
+        *pieces, kept = refs[-1 - PIECES :]
+        lefts = [left_in[slot] for slot in range(left_in.shape[0])]
         shift = shift_in[:, :1]
-    core, z = place[1], place[2]
+        if split:
+            partial = refs[3]
     block = held.shape[1] // 8
-    mask = 2 - core if swapped else 1 + core
-    for out, one, two, owner in ((sent, mask, 3 - mask, 1 - core), (kept, 3 - mask, mask, core)):
-        for index, flip in enumerate((two, 3) if first else (0, one)):
-            at = pl.ds(pl.multiple_of(((z ^ flip) * 2 + owner) * block, block), block)
-            product = 0.0
-            for slot, left in enumerate(lefts):
-                product = product + lax.dot_general(
-                    left, held[slot, at], (((1,), (1,)), ((), ())), preferred_element_type=F32
-                )
-            out[:, index * block : (index + 1) * block] = product * shrink - shift
-
-
-def apply_rows(first, factor, shrink, place, *arrays, after, swapped=False):
+    skip = 0 if first else 4
+    spans = blocks(place, held, swapped)[skip : skip + 4]
+    for index, at in enumerate(spans):
+        product = 0.0
+        if split:
+            low = (skip + index) * block
+            product = partial[:, low : low + block]
+        for slot, left in enumerate(lefts):
+            product = product + times(left, held, slot, at)
+        product = product * shrink - shift
+        outs, start = (pieces, index * block) if index < 2 else ([kept], (index - 2) * block)
+        width = outs[0].shape[1]
+        step = min(width, block)
+        for part in range(0, block, step):
+            place_in = start + part
+            outs[place_in // width][:, place_in % width : place_in % width + step] = product[:, part : part + step]
+
+
+def own_rows(factor, place, own, mean, scale, held, after, swapped=False):
+    many = own.shape[0]
+    return pl.pallas_call(
+        functools.partial(own_kernel, swapped, factor),
+        in_specs=[SMEM] + [VMEM] * 4 + [ANY] * len(after),
+        out_specs=[VMEM] * 2,
+        out_shape=[jax.ShapeDtypeStruct((many, held.shape[1]), F32), jax.ShapeDtypeStruct((many, 128), F32)],
+        compiler_params=pltpu.CompilerParams(vmem_limit_bytes=LIMIT),
+        cost_estimate=LIGHT,
+        name="own_rows",
+    )(place, own, mean, scale, *in_vmem(held), *after)
+
+
+def apply_rows(first, factor, shrink, place, *arrays, held, after, split=False, swapped=False):
     many = arrays[0].shape[-2]
-    held = arrays[-1]
+    place_of_held = 4 if first else 2
     wide = held.shape[1] // 4
-    out_shape = [jax.ShapeDtypeStruct((many, wide), F32)] * 2
+    out_shape = [jax.ShapeDtypeStruct((many, wide // PIECES), F32)] * PIECES
+    out_shape += [jax.ShapeDtypeStruct((many, wide), F32)]
     if first:
         out_shape += [
-            jax.ShapeDtypeStruct((2, many, held.shape[2]), jnp.bfloat16),
+            jax.ShapeDtypeStruct((1 if split else 2, many, held.shape[2]), jnp.bfloat16),
             jax.ShapeDtypeStruct((many, 128), F32),
         ]
     return pl.pallas_call(
-        functools.partial(apply_kernel, first, swapped, factor, shrink),
-        in_specs=[SMEM] + [VMEM] * len(arrays) + [ANY] * len(after),
+        functools.partial(apply_kernel, first, split, swapped, factor, shrink),
+        in_specs=[SMEM] + [VMEM] * (len(arrays) + 1) + [ANY] * len(after),
         out_specs=[VMEM] * len(out_shape),
         out_shape=out_shape,
         compiler_params=pltpu.CompilerParams(vmem_limit_bytes=LIMIT),
         cost_estimate=LIGHT,
         name="apply_first" if first else "apply_second",
-    )(place, *arrays[:-1], *in_vmem(held), *after)
+    )(place, *arrays[:place_of_held], *in_vmem(held), *arrays[place_of_held:], *after)
 
 
 def on_slice(dosage, allele_mean, allele_scale, probes):
@@ -247,23 +309,28 @@
     got_b = send(own_b, PLANE_SECOND)
     (own_a,) = add_up(own_a, got_a, after=[own_b])
     other_a = send(own_a, PLANE_FIRST)
-    (own_b,) = add_up(own_b, got_b, after=[own_a])
+    part_a, shift_a = own_rows(factor, place, own_a, mean, scale, held, after=[])
+    (own_b,) = add_up(own_b, got_b, after=[part_a])
     other_b = send(own_b, PLANE_FIRST)
-    sent, far_a, left, shift = apply_first(own_a, other_a, mean, scale, held, after=[own_b])
-    (far_a,) = add_up(far_a, send(sent, CORES))
+    *sent, far_a, left_a, shift_a = apply_first(
+        other_a, part_a, mean, scale, shift_a, held=held, after=[own_b], split=True
+    )
+    (far_a,) = add_up(far_a, *[send(piece, CORES) for piece in sent])
     got_a = send(far_a, LINE_FIRST)
-    sent, near_a = apply_second(left, shift, held, after=[far_a])
-    core_a = send(sent, CORES)
-    sent, far_b, left, shift = apply_first(own_b, other_b, mean, scale, held, after=[near_a], swapped=True)
-    core_b = send(sent, CORES)
+    *sent, near_a = apply_second(left_a, shift_a, part_a, held=held, after=[far_a], split=True)
+    core_a = [send(piece, CORES) for piece in sent]
+    *sent, far_b, left_b, shift_b = apply_first(
+        other_b, own_b, mean, scale, held=held, after=[near_a], swapped=True
+    )
+    (far_b,) = add_up(far_b, *[send(piece, CORES) for piece in sent])
+    got_b = send(far_b, LINE_SECOND)
     (near_a,) = add_up(near_a, got_a, after=[far_b])
-    near_a, sent_a = add_up(near_a, core_a, cut=2)
-    (far_b,) = add_up(far_b, core_b, after=[near_a])
-    got_a, got_b = send(sent_a, LINE_SECOND), send(far_b, LINE_SECOND)
-    sent, near_b = apply_second(left, shift, held, after=[far_b], swapped=True)
-    core_b = send(sent, CORES)
-    (near_b,) = add_up(near_b, got_b)
-    near_b, sent_b = add_up(near_b, core_b, cut=2)
+    near_a, sent_a = add_up(near_a, *core_a, cut=2)
+    got_a = send(sent_a, LINE_SECOND)
+    *sent, near_b = apply_second(left_b, shift_b, held=held, after=[near_a], swapped=True)
+    core_b = [send(piece, CORES) for piece in sent]
+    (near_b,) = add_up(near_b, got_b, after=[near_a])
+    near_b, sent_b = add_up(near_b, *core_b, cut=2)
     got_b = send(sent_b, LINE_FIRST)
     return jnp.concatenate([near_a + got_a, near_b + got_b], axis=0)
 

time: 72.8 us -> 69.7 us (0.957)
  waiting for transfers between devices: 26.6 us -> 21.4 us
  starting transfers between devices: 20.5 us -> 21.7 us
    ppermute x14 -> x18, waiting for transfers between devices: 26.6 us -> 21.4 us  [on_slice(): send = lambda array, moves: lax.ppermute(array, AXES, moves)]
    ppermute x14 -> x18, starting transfers between devices: 20.5 us -> 21.7 us  [on_slice(): send = lambda array, moves: lax.ppermute(array, AXES, moves)]
    pallas_call x4 -> x5, Pallas kernels: 13 us -> 13.7 us  [the longest x4 10.5 us: apply_rows(): pl.pallas_call(functools.partial(apply_kernel, first, split, swapped, fac...]
  transfers between devices with their start and end apart: 14 -> 18, of which waited for: 6 -> 11; matrix products, arithmetic and copies ran while one was open for 0% -> 0% of each run, Pallas kernels for 21% -> 28%
where the time goes in v3:
time: 69.7 us; the launch traced here: 68.6 us
  Pallas kernels  24.5 us (35%)
  starting transfers between devices  21.7 us (31%)
  waiting for transfers between devices  21.4 us (31%)
  other arithmetic  0.91 us (1%)
    ppermute x18, starting transfers between devices, on_slice(): send = lambda array, moves: lax.ppermute(array, AXES, moves)  21.7 us
    ppermute x18, waiting for transfers between devices, on_slice(): send = lambda array, moves: lax.ppermute(array, AXES, moves)  21.4 us
    pallas_call x4, Pallas kernels, apply_rows(): pl.pallas_call(functools.partial(apply_kernel, first, split, swapped, fac...  10.5 us
    pallas_call x1, Pallas kernels, first_half(): pl.pallas_call(functools.partial(loads_kernel, True), in_specs=[SMEM, HBM...  5.5 us
    pallas_call x1, Pallas kernels, second_half(): pl.pallas_call(functools.partial(loads_kernel, False), in_specs=[SMEM, VM...  4.85 us
    pallas_call x1, Pallas kernels, own_rows(): pl.pallas_call(functools.partial(own_kernel, swapped, factor), in_specs=[...  3.24 us
  transfers between devices with their start and end apart: 18, of which 11 were waited for; matrix products, arithmetic and copies ran while one was open for 0% of the time, Pallas kernels for 28%

profile of v3, /device:TPU:0, one launch (start us, length us, event | category | flops | bytes accessed | tf_op | source)
XLA Modules:
  0.0 68.6 jit_solution(694599838214151344)
XLA Ops:
  0.1 5.5 %loads_sent.1 = (f32[96,1024]{1,0:T(8,128)S(1)}, f32[96,1024]{1,0:T(8,128)S(1)}, bf16[192,4096]{1,0:T(8,128)(2,1)S(1)}, f32[192,128]{1,0:T(8,128)S(1)}, bf16[2,4096,1024]{2,1,0:T(8,128)(2,1)S(1)}) custom-call(s32[3]{0:T(128)S(1)} %pad_add_fusion.place, f32[192,4096]{1,0:T(8,128)} %probes.1, bf16[4096,2048]{1,0:T(8,128)(2,1)} %dosage.3, f32[1,2048]{1,0:T(1,128)} %bitcast.5), custom_call_target="tpu_custom_call" | custom-call | flops 1 | bytes 1 | tf_op jit(solution)/shard_map/loads_sent/pallas_call | solution.py:108
  5.6 3.0 %collective-permute-start = (f32[96,1024]{1,0:T(8,128)S(1)}, f32[96,1024]{1,0:T(8,128)S(1)}, u32[]{:S(2)}, u32[]{:S(2)}) collective-permute-start(f32[96,1024]{1,0:T(8,128)S(1)} %get-tuple-element.39), channel_id=1, source_target_pairs={{0,8},{1,17},{2,10},{3,19},{4,12},{5,21},{6,14},{7,23},{8,0},{9,25... | collective-permute-start | bytes 1179656 | tf_op jit(solution)/shard_map/ppermute | solution.py:298
  8.7 4.8 %loads_kept.1 = (f32[96,1024]{1,0:T(8,128)S(1)}, f32[96,1024]{1,0:T(8,128)S(1)}, bf16[2,4096,1024]{2,1,0:T(8,128)(2,1)S(1)}) custom-call(s32[3]{0:T(128)S(1)} %pad_add_fusion.place, bf16[192,4096]{1,0:T(8,128)(2,1)S(1)} %get-tuple-element.35.probes, bf16[4096,2048]{1,0:T(8,128)(2,1)} %dosage.3, ...), custom_call_target="tpu_custom_call", output_to_operand_aliasing={{2}: (5, {})} | custom-call | flops 1 | bytes 1 | tf_op jit(solution)/shard_map/loads_kept/pallas_call | solution.py:134
  13.5 0.8 %collective-permute-done.refs_1_ = f32[96,1024]{1,0:T(8,128)S(1)} collective-permute-done((f32[96,1024]{1,0:T(8,128)S(1)}, f32[96,1024]{1,0:T(8,128)S(1)}, u32[]{:S(2)}, u32[]{:S(2)}) %collective-permute-start) | collective-permute-done | bytes 393248 | tf_op jit(solution)/shard_map/ppermute | solution.py:298
  14.4 2.1 %collective-permute-start.1 = (f32[96,1024]{1,0:T(8,128)S(1)}, f32[96,1024]{1,0:T(8,128)S(1)}, u32[]{:S(2)}, u32[]{:S(2)}) collective-permute-start(f32[96,1024]{1,0:T(8,128)S(1)} %add_up.10.refs_2_.refs_0_), channel_id=1, source_target_pairs={{0,16},{1,9},{2,18},{3,11},{4,20},{5,13},{6,22},{7,15},{8,24},{9,1... | collective-permute-start | bytes 1179656 | tf_op jit(solution)/shard_map/ppermute | solution.py:298
  16.5 4.2 %collective-permute-done.2.refs_1_ = f32[96,1024]{1,0:T(8,128)S(1)} collective-permute-done((f32[96,1024]{1,0:T(8,128)S(1)}, f32[96,1024]{1,0:T(8,128)S(1)}, u32[]{:S(2)}, u32[]{:S(2)}) %collective-permute-start.2) | collective-permute-done | bytes 393248 | tf_op jit(solution)/shard_map/ppermute | solution.py:298
  20.7 2.4 %collective-permute-start.4 = (f32[96,1024]{1,0:T(8,128)S(1)}, f32[96,1024]{1,0:T(8,128)S(1)}, u32[]{:S(2)}, u32[]{:S(2)}) collective-permute-start(f32[96,1024]{1,0:T(8,128)S(1)} %add_up.11.refs_2_.refs_0_), channel_id=1, source_target_pairs={{0,16},{1,9},{2,18},{3,11},{4,20},{5,13},{6,22},{7,15},{8,24},{9,1... | collective-permute-start | bytes 1179656 | tf_op jit(solution)/shard_map/ppermute | solution.py:298
  23.2 1.6 %collective-permute-start.3 = (f32[96,1024]{1,0:T(8,128)S(1)}, f32[96,1024]{1,0:T(8,128)S(1)}, u32[]{:S(2)}, u32[]{:S(2)}) collective-permute-start(f32[96,1024]{1,0:T(8,128)S(1)} %add_up.12.own), channel_id=1, source_target_pairs={{0,8},{1,17},{2,10},{3,19},{4,12},{5,21},{6,14},{7,23},{8,0},{9,25... | collective-permute-start | bytes 1179656 | tf_op jit(solution)/shard_map/ppermute | solution.py:298
  24.8 3.2 %own_rows.1 = (f32[96,4096]{1,0:T(8,128)S(1)}, f32[96,128]{1,0:T(8,128)S(1)}) custom-call(s32[3]{0:T(128)S(1)} %pad_add_fusion.place, f32[96,1024]{1,0:T(8,128)S(1)} %add_up.12.own, f32[1,2048]{1,0:T(1,128)S(1)} %bitcast.7, f32[1,2048]{1,0:T(1,128)S(1)} %bitcast.10, bf16[2,4096,1024]{2,1,0:T(8,128)(2,1)S(1)} %get-tuple-element.42.held.refs_4_.refs_2_), custom_call_target="tpu_custom_call" | custom-call | flops 1 | bytes 1 | tf_op jit(solution)/shard_map/own_rows/pallas_call | solution.py:256
  28.0 4.2 %collective-permute-done.4.refs_1_ = f32[96,1024]{1,0:T(8,128)S(1)} collective-permute-done((f32[96,1024]{1,0:T(8,128)S(1)}, f32[96,1024]{1,0:T(8,128)S(1)}, u32[]{:S(2)}, u32[]{:S(2)}) %collective-permute-start.4) | collective-permute-done | bytes 393248 | tf_op jit(solution)/shard_map/ppermute | solution.py:298
  32.3 2.4 %collective-permute-start.8 = (f32[96,1024]{1,0:T(8,128)S(1)}, f32[96,1024]{1,0:T(8,128)S(1)}, u32[]{:S(2)}, u32[]{:S(2)}) collective-permute-start(f32[96,1024]{1,0:T(8,128)S(1)} %add_up.13.refs_6_.refs_1_), channel_id=1, source_target_pairs={{0,8},{1,17},{2,10},{3,19},{4,12},{5,21},{6,14},{7,23},{8,0},{9,25... | collective-permute-start | bytes 1179656 | tf_op jit(solution)/shard_map/ppermute | solution.py:298
  34.7 2.0 %apply_first.2 = (f32[96,512]{1,0:T(8,128)S(1)}, f32[96,512]{1,0:T(8,128)S(1)}, f32[96,1024]{1,0:T(8,128)S(1)}, bf16[1,96,1024]{2,1,0:T(8,128)(2,1)S(1)}, f32[96,128]{1,0:T(8,128)S(1)}) custom-call(s32[3]{0:T(128)S(1)} %pad_add_fusion.place, f32[96,1024]{1,0:T(8,128)S(1)} %collective-permute-done.3.refs_0_, ...), custom_call_target="tpu_custom_call" | custom-call | flops 1 | bytes 1 | tf_op jit(solution)/shard_map/apply_first/pallas_call | solution.py:278
  36.8 0.5 collective-permute-start.6
  37.3 0.9 %collective-permute-done.5.refs_1_ = f32[96,512]{1,0:T(8,128)S(1)} collective-permute-done((f32[96,512]{1,0:T(8,128)S(1)}, f32[96,512]{1,0:T(8,128)S(1)}, u32[]{:S(2)}, u32[]{:S(2)}) %collective-permute-start.5) | collective-permute-done | bytes 196640 | tf_op jit(solution)/shard_map/ppermute | solution.py:298
  38.2 0.3 collective-permute-done.6.refs_2_
  38.5 1.6 %collective-permute-start.7 = (f32[96,1024]{1,0:T(8,128)S(1)}, f32[96,1024]{1,0:T(8,128)S(1)}, u32[]{:S(2)}, u32[]{:S(2)}) collective-permute-start(f32[96,1024]{1,0:T(8,128)S(1)} %add_up.14.refs_4_), channel_id=1, source_target_pairs={{0,2},{1,5},{2,0},{3,7},{4,6},{5,1},{6,4},{7,3},{8,10},{9,13},{10,... | collective-permute-start | bytes 1179656 | tf_op jit(solution)/shard_map/ppermute | solution.py:298
  40.1 2.0 %apply_second.2 = (f32[96,512]{1,0:T(8,128)S(1)}, f32[96,512]{1,0:T(8,128)S(1)}, f32[96,1024]{1,0:T(8,128)S(1)}) custom-call(s32[3]{0:T(128)S(1)} %pad_add_fusion.place, bf16[1,96,1024]{2,1,0:T(8,128)(2,1)S(1)} %get-tuple-element.45.refs_0_, f32[96,128]{1,0:T(8,128)S(1)} %get-tuple-element.46.refs_1_, ...), custom_call_target="tpu_custom_call" | custom-call | flops 1 | bytes 1 | tf_op jit(solution)/shard_map/apply_second/pallas_call | solution.py:278
  42.1 3.3 %apply_first.3 = (f32[96,512]{1,0:T(8,128)S(1)}, f32[96,512]{1,0:T(8,128)S(1)}, f32[96,1024]{1,0:T(8,128)S(1)}, bf16[2,96,1024]{2,1,0:T(8,128)(2,1)S(1)}, f32[96,128]{1,0:T(8,128)S(1)}) custom-call(s32[3]{0:T(128)S(1)} %pad_add_fusion.place, f32[96,1024]{1,0:T(8,128)S(1)} %collective-permute-done.8.refs_0_, f32[96,1024]{1,0:T(8,128)S(1)} %add_up.13.refs_6_.refs_1_, ...), custom_call_target="tpu_custom_call" | custom-call | flops 1 | bytes 1 | tf_op jit(solution)/shard_map/apply_first/pallas_call | solution.py:278
  45.4 1.0 %collective-permute-start.9 = (f32[96,512]{1,0:T(8,128)S(1)}, f32[96,512]{1,0:T(8,128)S(1)}, u32[]{:S(2)}, u32[]{:S(2)}) collective-permute-start(f32[96,512]{1,0:T(8,128)S(1)} %get-tuple-element.52), channel_id=1, source_target_pairs={{0,1},{1,0},{2,3},{3,2},{4,5},{5,4},{6,7},{7,6},{8,9},{9,8},{10,11... | collective-permute-start | bytes 589832 | tf_op jit(solution)/shard_map/ppermute | solution.py:298
  46.5 0.4 collective-permute-start.11
  47.0 0.5 collective-permute-done.9.refs_1_
  47.5 0.4 collective-permute-done.10.refs_2_
  47.9 2.0 %collective-permute-start.14 = (f32[96,1024]{1,0:T(8,128)S(1)}, f32[96,1024]{1,0:T(8,128)S(1)}, u32[]{:S(2)}, u32[]{:S(2)}) collective-permute-start(f32[96,1024]{1,0:T(8,128)S(1)} %add_up.15.refs_2_), channel_id=1, source_target_pairs={{0,4},{1,3},{2,6},{3,1},{4,0},{5,7},{6,2},{7,5},{8,12},{9,11},{10,... | collective-permute-start | bytes 1179656 | tf_op jit(solution)/shard_map/ppermute | solution.py:298
  49.9 0.6 collective-permute-done.7.refs_1_
  50.6 3.2 %apply_second.3 = (f32[96,512]{1,0:T(8,128)S(1)}, f32[96,512]{1,0:T(8,128)S(1)}, f32[96,1024]{1,0:T(8,128)S(1)}) custom-call(s32[3]{0:T(128)S(1)} %pad_add_fusion.place, bf16[2,96,1024]{2,1,0:T(8,128)(2,1)S(1)} %get-tuple-element.58.refs_0_, f32[96,128]{1,0:T(8,128)S(1)} %get-tuple-element.59.refs_1_, ...), custom_call_target="tpu_custom_call" | custom-call | flops 1 | bytes 1 | tf_op jit(solution)/shard_map/apply_second/pallas_call | solution.py:278
  53.9 0.5 collective-permute-start.16
  54.4 3.4 %collective-permute-start.13 = (f32[96,512]{1,0:T(8,128)S(1)}, f32[96,512]{1,0:T(8,128)S(1)}, u32[]{:S(2)}, u32[]{:S(2)}) collective-permute-start(f32[96,512]{1,0:T(8,128)S(1)} %get-tuple-element.57), channel_id=1, source_target_pairs={{0,4},{1,3},{2,6},{3,1},{4,0},{5,7},{6,2},{7,5},{8,12},{9,11},{10,... | collective-permute-start | bytes 589832 | tf_op jit(solution)/shard_map/ppermute | solution.py:298
  57.8 3.2 %collective-permute-done.14.refs_1_ = f32[96,1024]{1,0:T(8,128)S(1)} collective-permute-done((f32[96,1024]{1,0:T(8,128)S(1)}, f32[96,1024]{1,0:T(8,128)S(1)}, u32[]{:S(2)}, u32[]{:S(2)}) %collective-permute-start.14) | collective-permute-done | bytes 393248 | tf_op jit(solution)/shard_map/ppermute | solution.py:298
  61.2 0.3 collective-permute-start.17
  61.4 6.0 %collective-permute-done.13 = f32[96,512]{1,0:T(8,128)S(1)} collective-permute-done((f32[96,512]{1,0:T(8,128)S(1)}, f32[96,512]{1,0:T(8,128)S(1)}, u32[]{:S(2)}, u32[]{:S(2)}) %collective-permute-start.13) | collective-permute-done | bytes 196640 | tf_op jit(solution)/shard_map/ppermute | solution.py:298
  67.5 0.3 collective-permute-done.17
  67.8 0.8 %pad_maximum_fusion = f32[192,512]{1,0:T(8,128)} fusion(f32[96,512]{1,0:T(8,128)S(1)} %add.18, f32[96,512]{1,0:T(8,128)S(1)} %add.17), kind=kLoop, calls=%fused_computation | loop fusion | flops 98304 | bytes 786432 | tf_op jit(solution)/shard_map/concatenate | solution.py:335
  (29 shorter events, 1.0 us)
Async XLA Ops:
  0.0 8.7 %copy-start = (f32[2048]{0:T(1024)S(1)}, f32[2048]{0:T(1024)}, u32[]{:S(2)}) copy-start(f32[2048]{0:T(1024)} %param.5) | copy-start | bytes 24580
  5.6 8.8 %collective-permute-start = (f32[96,1024]{1,0:T(8,128)S(1)}, f32[96,1024]{1,0:T(8,128)S(1)}, u32[]{:S(2)}, u32[]{:S(2)}) collective-permute-start(f32[96,1024]{1,0:T(8,128)S(1)} %get-tuple-element.39), channel_id=1, source_target_pairs={{0,8},{1,17},{2,10},{3,19},{4,12},{5,21},{6,14},{7,23},{8,0},{9,25... | collective-permute-start | bytes 1179656 | tf_op jit(solution)/shard_map/ppermute | solution.py:298
  8.6 12.1 %collective-permute-start.2 = (f32[96,1024]{1,0:T(8,128)S(1)}, f32[96,1024]{1,0:T(8,128)S(1)}, u32[]{:S(2)}, u32[]{:S(2)}) collective-permute-start(f32[96,1024]{1,0:T(8,128)S(1)} %get-tuple-element.41), channel_id=1, source_target_pairs={{0,8},{1,17},{2,10},{3,19},{4,12},{5,21},{6,14},{7,23},{8,0},{9,25... | collective-permute-start | bytes 1179656 | tf_op jit(solution)/shard_map/ppermute | solution.py:298
  8.7 16.1 %copy-start.1 = (f32[2048]{0:T(1024)S(1)}, f32[2048]{0:T(1024)}, u32[]{:S(2)}) copy-start(f32[2048]{0:T(1024)} %param.6) | copy-start | bytes 24580
  14.4 8.8 %collective-permute-start.1 = (f32[96,1024]{1,0:T(8,128)S(1)}, f32[96,1024]{1,0:T(8,128)S(1)}, u32[]{:S(2)}, u32[]{:S(2)}) collective-permute-start(f32[96,1024]{1,0:T(8,128)S(1)} %add_up.10.refs_2_.refs_0_), channel_id=1, source_target_pairs={{0,16},{1,9},{2,18},{3,11},{4,20},{5,13},{6,22},{7,15},{8,24},{9,1... | collective-permute-start | bytes 1179656 | tf_op jit(solution)/shard_map/ppermute | solution.py:298
  20.7 11.5 %collective-permute-start.4 = (f32[96,1024]{1,0:T(8,128)S(1)}, f32[96,1024]{1,0:T(8,128)S(1)}, u32[]{:S(2)}, u32[]{:S(2)}) collective-permute-start(f32[96,1024]{1,0:T(8,128)S(1)} %add_up.11.refs_2_.refs_0_), channel_id=1, source_target_pairs={{0,16},{1,9},{2,18},{3,11},{4,20},{5,13},{6,22},{7,15},{8,24},{9,1... | collective-permute-start | bytes 1179656 | tf_op jit(solution)/shard_map/ppermute | solution.py:298
  23.2 11.5 %collective-permute-start.3 = (f32[96,1024]{1,0:T(8,128)S(1)}, f32[96,1024]{1,0:T(8,128)S(1)}, u32[]{:S(2)}, u32[]{:S(2)}) collective-permute-start(f32[96,1024]{1,0:T(8,128)S(1)} %add_up.12.own), channel_id=1, source_target_pairs={{0,8},{1,17},{2,10},{3,19},{4,12},{5,21},{6,14},{7,23},{8,0},{9,25... | collective-permute-start | bytes 1179656 | tf_op jit(solution)/shard_map/ppermute | solution.py:298
  32.3 9.8 %collective-permute-start.8 = (f32[96,1024]{1,0:T(8,128)S(1)}, f32[96,1024]{1,0:T(8,128)S(1)}, u32[]{:S(2)}, u32[]{:S(2)}) collective-permute-start(f32[96,1024]{1,0:T(8,128)S(1)} %add_up.13.refs_6_.refs_1_), channel_id=1, source_target_pairs={{0,8},{1,17},{2,10},{3,19},{4,12},{5,21},{6,14},{7,23},{8,0},{9,25... | collective-permute-start | bytes 1179656 | tf_op jit(solution)/shard_map/ppermute | solution.py:298
  36.7 1.5 %collective-permute-start.5 = (f32[96,512]{1,0:T(8,128)S(1)}, f32[96,512]{1,0:T(8,128)S(1)}, u32[]{:S(2)}, u32[]{:S(2)}) collective-permute-start(f32[96,512]{1,0:T(8,128)S(1)} %get-tuple-element.48), channel_id=1, source_target_pairs={{0,1},{1,0},{2,3},{3,2},{4,5},{5,4},{6,7},{7,6},{8,9},{9,8},{10,11... | collective-permute-start | bytes 589832 | tf_op jit(solution)/shard_map/ppermute | solution.py:298
  36.8 1.7 %collective-permute-start.6 = (f32[96,512]{1,0:T(8,128)S(1)}, f32[96,512]{1,0:T(8,128)S(1)}, u32[]{:S(2)}, u32[]{:S(2)}) collective-permute-start(f32[96,512]{1,0:T(8,128)S(1)} %get-tuple-element.49), channel_id=1, source_target_pairs={{0,1},{1,0},{2,3},{3,2},{4,5},{5,4},{6,7},{7,6},{8,9},{9,8},{10,11... | collective-permute-start | bytes 589832 | tf_op jit(solution)/shard_map/ppermute | solution.py:298
  38.5 12.0 %collective-permute-start.7 = (f32[96,1024]{1,0:T(8,128)S(1)}, f32[96,1024]{1,0:T(8,128)S(1)}, u32[]{:S(2)}, u32[]{:S(2)}) collective-permute-start(f32[96,1024]{1,0:T(8,128)S(1)} %add_up.14.refs_4_), channel_id=1, source_target_pairs={{0,2},{1,5},{2,0},{3,7},{4,6},{5,1},{6,4},{7,3},{8,10},{9,13},{10,... | collective-permute-start | bytes 1179656 | tf_op jit(solution)/shard_map/ppermute | solution.py:298
  45.4 2.1 %collective-permute-start.9 = (f32[96,512]{1,0:T(8,128)S(1)}, f32[96,512]{1,0:T(8,128)S(1)}, u32[]{:S(2)}, u32[]{:S(2)}) collective-permute-start(f32[96,512]{1,0:T(8,128)S(1)} %get-tuple-element.52), channel_id=1, source_target_pairs={{0,1},{1,0},{2,3},{3,2},{4,5},{5,4},{6,7},{7,6},{8,9},{9,8},{10,11... | collective-permute-start | bytes 589832 | tf_op jit(solution)/shard_map/ppermute | solution.py:298
  46.5 1.4 %collective-permute-start.10 = (f32[96,512]{1,0:T(8,128)S(1)}, f32[96,512]{1,0:T(8,128)S(1)}, u32[]{:S(2)}, u32[]{:S(2)}) collective-permute-start(f32[96,512]{1,0:T(8,128)S(1)} %get-tuple-element.53), channel_id=1, source_target_pairs={{0,1},{1,0},{2,3},{3,2},{4,5},{5,4},{6,7},{7,6},{8,9},{9,8},{10,11... | collective-permute-start | bytes 589832 | tf_op jit(solution)/shard_map/ppermute | solution.py:298
  46.5 4.0 %collective-permute-start.11 = (f32[96,512]{1,0:T(8,128)S(1)}, f32[96,512]{1,0:T(8,128)S(1)}, u32[]{:S(2)}, u32[]{:S(2)}) collective-permute-start(f32[96,512]{1,0:T(8,128)S(1)} %get-tuple-element.54), channel_id=1, source_target_pairs={{0,1},{1,0},{2,3},{3,2},{4,5},{5,4},{6,7},{7,6},{8,9},{9,8},{10,11... | collective-permute-start | bytes 589832 | tf_op jit(solution)/shard_map/ppermute | solution.py:298
  47.0 3.6 %collective-permute-start.12 = (f32[96,512]{1,0:T(8,128)S(1)}, f32[96,512]{1,0:T(8,128)S(1)}, u32[]{:S(2)}, u32[]{:S(2)}) collective-permute-start(f32[96,512]{1,0:T(8,128)S(1)} %get-tuple-element.55), channel_id=1, source_target_pairs={{0,1},{1,0},{2,3},{3,2},{4,5},{5,4},{6,7},{7,6},{8,9},{9,8},{10,11... | collective-permute-start | bytes 589832 | tf_op jit(solution)/shard_map/ppermute | solution.py:298
  47.9 13.1 %collective-permute-start.14 = (f32[96,1024]{1,0:T(8,128)S(1)}, f32[96,1024]{1,0:T(8,128)S(1)}, u32[]{:S(2)}, u32[]{:S(2)}) collective-permute-start(f32[96,1024]{1,0:T(8,128)S(1)} %add_up.15.refs_2_), channel_id=1, source_target_pairs={{0,4},{1,3},{2,6},{3,1},{4,0},{5,7},{6,2},{7,5},{8,12},{9,11},{10,... | collective-permute-start | bytes 1179656 | tf_op jit(solution)/shard_map/ppermute | solution.py:298
  53.8 7.2 %collective-permute-start.15 = (f32[96,512]{1,0:T(8,128)S(1)}, f32[96,512]{1,0:T(8,128)S(1)}, u32[]{:S(2)}, u32[]{:S(2)}) collective-permute-start(f32[96,512]{1,0:T(8,128)S(1)} %get-tuple-element.61), channel_id=1, source_target_pairs={{0,1},{1,0},{2,3},{3,2},{4,5},{5,4},{6,7},{7,6},{8,9},{9,8},{10,11... | collective-permute-start | bytes 589832 | tf_op jit(solution)/shard_map/ppermute | solution.py:298
  53.9 7.2 %collective-permute-start.16 = (f32[96,512]{1,0:T(8,128)S(1)}, f32[96,512]{1,0:T(8,128)S(1)}, u32[]{:S(2)}, u32[]{:S(2)}) collective-permute-start(f32[96,512]{1,0:T(8,128)S(1)} %get-tuple-element.62), channel_id=1, source_target_pairs={{0,1},{1,0},{2,3},{3,2},{4,5},{5,4},{6,7},{7,6},{8,9},{9,8},{10,11... | collective-permute-start | bytes 589832 | tf_op jit(solution)/shard_map/ppermute | solution.py:298
  54.4 13.0 %collective-permute-start.13 = (f32[96,512]{1,0:T(8,128)S(1)}, f32[96,512]{1,0:T(8,128)S(1)}, u32[]{:S(2)}, u32[]{:S(2)}) collective-permute-start(f32[96,512]{1,0:T(8,128)S(1)} %get-tuple-element.57), channel_id=1, source_target_pairs={{0,4},{1,3},{2,6},{3,1},{4,0},{5,7},{6,2},{7,5},{8,12},{9,11},{10,... | collective-permute-start | bytes 589832 | tf_op jit(solution)/shard_map/ppermute | solution.py:298
  61.2 6.6 %collective-permute-start.17 = (f32[96,512]{1,0:T(8,128)S(1)}, f32[96,512]{1,0:T(8,128)S(1)}, u32[]{:S(2)}, u32[]{:S(2)}) collective-permute-start(f32[96,512]{1,0:T(8,128)S(1)} %get-tuple-element.64), channel_id=1, source_target_pairs={{0,2},{1,5},{2,0},{3,7},{4,6},{5,1},{6,4},{7,3},{8,10},{9,13},{10,... | collective-permute-start | bytes 589832 | tf_op jit(solution)/shard_map/ppermute | solution.py:298

commit v4 on v3

--- a/solution.py
+++ b/solution.py
@@ -8,7 +8,7 @@
 from jax.sharding import PartitionSpec as P
 
 AXES = ("sample", "snp")
-CHUNKS = (96, 96)
+CHUNKS = (112, 80)
 STEPS = 8
 PIECES = 2
 LIMIT = 20 * 1024 * 1024
@@ -176,8 +176,31 @@
     )(*arrays, *after)
 
 
-def scaled(ref, gain, middle, factor):
-    left = (ref[...] * (gain * gain * factor)).astype(jnp.bfloat16)
+def halves_kernel(count, *refs):
+    whole, received, (out, *halves) = refs[0], refs[1 : 1 + count], refs[-3:]
+    width = halves[0].shape[1]
+    for index, half in enumerate(halves):
+        at = slice(index * width, (index + 1) * width)
+        value = whole[:, at] + (received[0][:, at] if count == 1 else received[index][...])
+        out[:, at] = value
+        half[...] = value
+
+
+def add_halves(whole, received, after=()):
+    many, width = whole.shape
+    return pl.pallas_call(
+        functools.partial(halves_kernel, len(received)),
+        in_specs=[VMEM] * (1 + len(received)) + [ANY] * len(after),
+        out_specs=[VMEM] * 3,
+        out_shape=[jax.ShapeDtypeStruct((many, wide), F32) for wide in (width, width // 2, width // 2)],
+        compiler_params=pltpu.CompilerParams(vmem_limit_bytes=LIMIT),
+        cost_estimate=LIGHT,
+        name="add_halves",
+    )(whole, *received, *after)
+
+
+def scaled(loads, gain, middle, factor):
+    left = (loads * (gain * gain * factor)).astype(jnp.bfloat16)
     return left, jnp.sum(left.astype(F32) * middle, axis=1, keepdims=True)
 
 
@@ -201,7 +224,7 @@
 def own_kernel(swapped, factor, place, own, mean, scale, held, *refs):
     partial, shift_out = refs[-2:]
     span = half_span(place[0], own.shape[1])
-    left, shift = scaled(own, scale[:, span], mean[:, span], factor)
+    left, shift = scaled(own[...], scale[:, span], mean[:, span], factor)
     shift_out[...] = jnp.broadcast_to(shift, shift_out.shape)
     block = held.shape[1] // 8
     for index, at in enumerate(blocks(place, held, swapped)):
@@ -212,6 +235,9 @@
     if first:
         other, own, mean, scale, held = refs[:5]
         *pieces, kept, left_out, shift_out = refs[-3 - PIECES :]
+        other = other[...]
+        if split:
+            other = jnp.concatenate([other, refs[6][...]], axis=1)
         span = half_span(1 - place[0], other.shape[1])
         left, shift = scaled(other, scale[:, span], mean[:, span], factor)
         left_out[0] = left
@@ -220,7 +246,7 @@
             partial, shift_own = own, refs[5][:, :1]
         else:
             span = half_span(place[0], own.shape[1])
-            left, shift_own = scaled(own, scale[:, span], mean[:, span], factor)
+            left, shift_own = scaled(own[...], scale[:, span], mean[:, span], factor)
             left_out[1] = left
             lefts.append(left)
         shift = (shift + shift_own) * shrink
@@ -303,17 +329,17 @@
     sent_a, sent_b, probe_b, sums, held = first_half(place, probes, dosage, mean)
     got_a, got_b = send(sent_a, PLANE_FIRST), send(sent_b, PLANE_FIRST)
     own_a, own_b, held = second_half(place, probe_b, dosage, mean, sums, held)
-    (own_a,) = add_up(own_a, got_a)
-    got_a = send(own_a, PLANE_SECOND)
+    own_a, *parts = add_halves(own_a, [got_a])
+    got_a = [send(part, PLANE_SECOND) for part in parts]
     (own_b,) = add_up(own_b, got_b, after=[own_a])
     got_b = send(own_b, PLANE_SECOND)
-    (own_a,) = add_up(own_a, got_a, after=[own_b])
-    other_a = send(own_a, PLANE_FIRST)
+    own_a, *parts = add_halves(own_a, got_a, after=[own_b])
+    other_a = [send(part, PLANE_FIRST) for part in parts]
     part_a, shift_a = own_rows(factor, place, own_a, mean, scale, held, after=[])
     (own_b,) = add_up(own_b, got_b, after=[part_a])
     other_b = send(own_b, PLANE_FIRST)
     *sent, far_a, left_a, shift_a = apply_first(
-        other_a, part_a, mean, scale, shift_a, held=held, after=[own_b], split=True
+        other_a[0], part_a, mean, scale, shift_a, other_a[1], held=held, after=[own_b], split=True
     )
     (far_a,) = add_up(far_a, *[send(piece, CORES) for piece in sent])
     got_a = send(far_a, LINE_FIRST)

time: 69.7 us -> 68.2 us (0.978); the launches traced: 68.6 us -> 68.1 us
  waiting for transfers between devices: 21.4 us -> 18.4 us
  starting transfers between devices: 21.7 us -> 24 us
    ppermute x18 -> x20, waiting for transfers between devices: 21.4 us -> 18.4 us  [on_slice(): send = lambda array, moves: lax.ppermute(array, AXES, moves)]
    ppermute x18 -> x20, starting transfers between devices: 21.7 us -> 24 us  [on_slice(): send = lambda array, moves: lax.ppermute(array, AXES, moves)]
  transfers between devices with their start and end apart: 18 -> 20, of which waited for: 11 -> 11; matrix products, arithmetic and copies ran while one was open for 0% -> 0% of each run, Pallas kernels for 28% -> 25%
where the time goes in v4:
time: 68.2 us; the launch traced here: 68.1 us
  Pallas kernels  24.6 us (36%)
  starting transfers between devices  24 us (35%)
  waiting for transfers between devices  18.4 us (27%)
  other arithmetic  0.91 us (1%)
    ppermute x20, starting transfers between devices, on_slice(): send = lambda array, moves: lax.ppermute(array, AXES, moves)  24 us
    ppermute x20, waiting for transfers between devices, on_slice(): send = lambda array, moves: lax.ppermute(array, AXES, moves)  18.4 us
    pallas_call x4, Pallas kernels, apply_rows(): pl.pallas_call(functools.partial(apply_kernel, first, split, swapped, fac...  10.5 us
    pallas_call x1, Pallas kernels, first_half(): pl.pallas_call(functools.partial(loads_kernel, True), in_specs=[SMEM, HBM...  5.5 us
    pallas_call x1, Pallas kernels, second_half(): pl.pallas_call(functools.partial(loads_kernel, False), in_specs=[SMEM, VM...  4.83 us
    pallas_call x1, Pallas kernels, own_rows(): pl.pallas_call(functools.partial(own_kernel, swapped, factor), in_specs=[...  3.33 us
  transfers between devices with their start and end apart: 20, of which 11 were waited for; matrix products, arithmetic and copies ran while one was open for 0% of the time, Pallas kernels for 25%

profile of v4, /device:TPU:0, one launch (start us, length us, event | category | flops | bytes accessed | tf_op | source)
XLA Modules:
  0.0 68.1 jit_solution(1909572500497610029)
XLA Ops:
  0.1 5.5 %loads_sent.1 = (f32[112,1024]{1,0:T(8,128)S(1)}, f32[80,1024]{1,0:T(8,128)S(1)}, bf16[192,4096]{1,0:T(8,128)(2,1)S(1)}, f32[192,128]{1,0:T(8,128)S(1)}, bf16[2,4096,1024]{2,1,0:T(8,128)(2,1)S(1)}) custom-call(s32[3]{0:T(128)S(1)} %pad_add_fusion.place, f32[192,4096]{1,0:T(8,128)} %probes.1, bf16[4096,2048]{1,0:T(8,128)(2,1)} %dosage.3, f32[1,2048]{1,0:T(1,128)} %bitcast.5), custom_call_target="tpu_custom_call" | custom-call | flops 1 | bytes 1 | tf_op jit(solution)/shard_map/loads_sent/pallas_call | solution.py:108
  5.6 3.0 %collective-permute-start = (f32[112,1024]{1,0:T(8,128)S(1)}, f32[112,1024]{1,0:T(8,128)S(1)}, u32[]{:S(2)}, u32[]{:S(2)}) collective-permute-start(f32[112,1024]{1,0:T(8,128)S(1)} %get-tuple-element.45), channel_id=1, source_target_pairs={{0,8},{1,17},{2,10},{3,19},{4,12},{5,21},{6,14},{7,23},{8,0},{9,25... | collective-permute-start | bytes 1376264 | tf_op jit(solution)/shard_map/ppermute | solution.py:324
  8.7 4.8 %loads_kept.1 = (f32[112,1024]{1,0:T(8,128)S(1)}, f32[80,1024]{1,0:T(8,128)S(1)}, bf16[2,4096,1024]{2,1,0:T(8,128)(2,1)S(1)}) custom-call(s32[3]{0:T(128)S(1)} %pad_add_fusion.place, bf16[192,4096]{1,0:T(8,128)(2,1)S(1)} %get-tuple-element.41.probes, bf16[4096,2048]{1,0:T(8,128)(2,1)} %dosage.3, ...), custom_call_target="tpu_custom_call", output_to_operand_aliasing={{2}: (5, {})} | custom-call | flops 1 | bytes 1 | tf_op jit(solution)/shard_map/loads_kept/pallas_call | solution.py:134
  13.5 1.5 %collective-permute-done.refs_1_ = f32[112,1024]{1,0:T(8,128)S(1)} collective-permute-done((f32[112,1024]{1,0:T(8,128)S(1)}, f32[112,1024]{1,0:T(8,128)S(1)}, u32[]{:S(2)}, u32[]{:S(2)}) %collective-permute-start) | collective-permute-done | bytes 458784 | tf_op jit(solution)/shard_map/ppermute | solution.py:324
  15.1 2.1 %collective-permute-start.1 = (f32[112,512]{1,0:T(8,128)S(1)}, f32[112,512]{1,0:T(8,128)S(1)}, u32[]{:S(2)}, u32[]{:S(2)}) collective-permute-start(f32[112,512]{1,0:T(8,128)S(1)} %get-tuple-element.47), channel_id=1, source_target_pairs={{0,16},{1,9},{2,18},{3,11},{4,20},{5,13},{6,22},{7,15},{8,24},{9,1... | collective-permute-start | bytes 688136 | tf_op jit(solution)/shard_map/ppermute | solution.py:324
  17.3 2.7 %collective-permute-done.3.refs_1_ = f32[80,1024]{1,0:T(8,128)S(1)} collective-permute-done((f32[80,1024]{1,0:T(8,128)S(1)}, f32[80,1024]{1,0:T(8,128)S(1)}, u32[]{:S(2)}, u32[]{:S(2)}) %collective-permute-start.3) | collective-permute-done | bytes 327712 | tf_op jit(solution)/shard_map/ppermute | solution.py:324
  20.0 2.4 %collective-permute-start.6 = (f32[80,1024]{1,0:T(8,128)S(1)}, f32[80,1024]{1,0:T(8,128)S(1)}, u32[]{:S(2)}, u32[]{:S(2)}) collective-permute-start(f32[80,1024]{1,0:T(8,128)S(1)} %add_up.8.refs_3_.refs_0_), channel_id=1, source_target_pairs={{0,16},{1,9},{2,18},{3,11},{4,20},{5,13},{6,22},{7,15},{8,24},{9,1... | collective-permute-start | bytes 983048 | tf_op jit(solution)/shard_map/ppermute | solution.py:324
  22.5 1.2 %collective-permute-done.2.refs_2_ = f32[112,512]{1,0:T(8,128)S(1)} collective-permute-done((f32[112,512]{1,0:T(8,128)S(1)}, f32[112,512]{1,0:T(8,128)S(1)}, u32[]{:S(2)}, u32[]{:S(2)}) %collective-permute-start.2) | collective-permute-done | bytes 229408 | tf_op jit(solution)/shard_map/ppermute | solution.py:324
  23.8 2.1 %collective-permute-start.4 = (f32[112,512]{1,0:T(8,128)S(1)}, f32[112,512]{1,0:T(8,128)S(1)}, u32[]{:S(2)}, u32[]{:S(2)}) collective-permute-start(f32[112,512]{1,0:T(8,128)S(1)} %get-tuple-element.51), channel_id=1, source_target_pairs={{0,8},{1,17},{2,10},{3,19},{4,12},{5,21},{6,14},{7,23},{8,0},{9,25... | collective-permute-start | bytes 688136 | tf_op jit(solution)/shard_map/ppermute | solution.py:324
  25.9 3.3 %own_rows.1 = (f32[112,4096]{1,0:T(8,128)S(1)}, f32[112,128]{1,0:T(8,128)S(1)}) custom-call(s32[3]{0:T(128)S(1)} %pad_add_fusion.place, f32[112,1024]{1,0:T(8,128)S(1)} %get-tuple-element.52.own, f32[1,2048]{1,0:T(1,128)S(1)} %bitcast.7, f32[1,2048]{1,0:T(1,128)S(1)} %bitcast.10, bf16[2,4096,1024]{2,1,0:T(8,128)(2,1)S(1)} %get-tuple-element.53.held.refs_4_.refs_2_), custom_call_target="tpu_custom_call" | custom-call | flops 1 | bytes 1 | tf_op jit(solution)/shard_map/own_rows/pallas_call | solution.py:282
  29.3 0.5 collective-permute-done.4.refs_0_
  29.8 2.5 %collective-permute-done.5.refs_6_ = f32[112,512]{1,0:T(8,128)S(1)} collective-permute-done((f32[112,512]{1,0:T(8,128)S(1)}, f32[112,512]{1,0:T(8,128)S(1)}, u32[]{:S(2)}, u32[]{:S(2)}) %collective-permute-start.5) | collective-permute-done | bytes 229408 | tf_op jit(solution)/shard_map/ppermute | solution.py:324
  32.3 2.0 %apply_first.2 = (f32[112,512]{1,0:T(8,128)S(1)}, f32[112,512]{1,0:T(8,128)S(1)}, f32[112,1024]{1,0:T(8,128)S(1)}, bf16[1,112,1024]{2,1,0:T(8,128)(2,1)S(1)}, f32[112,128]{1,0:T(8,128)S(1)}) custom-call(s32[3]{0:T(128)S(1)} %pad_add_fusion.place, f32[112,512]{1,0:T(8,128)S(1)} %collective-permute-done.4.refs_0_, ...), custom_call_target="tpu_custom_call" | custom-call | flops 1 | bytes 1 | tf_op jit(solution)/shard_map/apply_first/pallas_call | solution.py:304
  34.5 0.4 collective-permute-start.8
  34.9 2.0 %collective-permute-start.10 = (f32[80,1024]{1,0:T(8,128)S(1)}, f32[80,1024]{1,0:T(8,128)S(1)}, u32[]{:S(2)}, u32[]{:S(2)}) collective-permute-start(f32[80,1024]{1,0:T(8,128)S(1)} %add_up.9.refs_7_.refs_1_), channel_id=1, source_target_pairs={{0,8},{1,17},{2,10},{3,19},{4,12},{5,21},{6,14},{7,23},{8,0},{9,25... | collective-permute-start | bytes 983048 | tf_op jit(solution)/shard_map/ppermute | solution.py:324
  37.0 1.6 %collective-permute-start.9 = (f32[112,1024]{1,0:T(8,128)S(1)}, f32[112,1024]{1,0:T(8,128)S(1)}, u32[]{:S(2)}, u32[]{:S(2)}) collective-permute-start(f32[112,1024]{1,0:T(8,128)S(1)} %add_up.10.refs_4_), channel_id=1, source_target_pairs={{0,2},{1,5},{2,0},{3,7},{4,6},{5,1},{6,4},{7,3},{8,10},{9,13},{10,... | collective-permute-start | bytes 1376264 | tf_op jit(solution)/shard_map/ppermute | solution.py:324
  38.6 2.0 %apply_second.2 = (f32[112,512]{1,0:T(8,128)S(1)}, f32[112,512]{1,0:T(8,128)S(1)}, f32[112,1024]{1,0:T(8,128)S(1)}) custom-call(s32[3]{0:T(128)S(1)} %pad_add_fusion.place, bf16[1,112,1024]{2,1,0:T(8,128)(2,1)S(1)} %get-tuple-element.57.refs_0_, f32[112,128]{1,0:T(8,128)S(1)} %get-tuple-element.58.refs_1_, ...), custom_call_target="tpu_custom_call" | custom-call | flops 1 | bytes 1 | tf_op jit(solution)/shard_map/apply_second/pallas_call | solution.py:304
  40.6 1.3 %collective-permute-done.10.refs_0_ = f32[80,1024]{1,0:T(8,128)S(1)} collective-permute-done((f32[80,1024]{1,0:T(8,128)S(1)}, f32[80,1024]{1,0:T(8,128)S(1)}, u32[]{:S(2)}, u32[]{:S(2)}) %collective-permute-start.10) | collective-permute-done | bytes 327712 | tf_op jit(solution)/shard_map/ppermute | solution.py:324
  42.0 3.2 %apply_first.3 = (f32[80,512]{1,0:T(8,128)S(1)}, f32[80,512]{1,0:T(8,128)S(1)}, f32[80,1024]{1,0:T(8,128)S(1)}, bf16[2,80,1024]{2,1,0:T(8,128)(2,1)S(1)}, f32[80,128]{1,0:T(8,128)S(1)}) custom-call(s32[3]{0:T(128)S(1)} %pad_add_fusion.place, f32[80,1024]{1,0:T(8,128)S(1)} %collective-permute-done.10.refs_0_, f32[80,1024]{1,0:T(8,128)S(1)} %add_up.9.refs_7_.refs_1_, ...), custom_call_target="tpu_custom_call" | custom-call | flops 1 | bytes 1 | tf_op jit(solution)/shard_map/apply_first/pallas_call | solution.py:304
  45.3 0.5 collective-permute-start.12
  45.9 0.4 collective-permute-start.14
  46.3 0.4 collective-permute-done.11.refs_1_
  46.7 0.2 collective-permute-done.12.refs_2_
  46.9 3.2 %collective-permute-start.16 = (f32[80,1024]{1,0:T(8,128)S(1)}, f32[80,1024]{1,0:T(8,128)S(1)}, u32[]{:S(2)}, u32[]{:S(2)}) collective-permute-start(f32[80,1024]{1,0:T(8,128)S(1)} %add_up.11.refs_2_), channel_id=1, source_target_pairs={{0,4},{1,3},{2,6},{3,1},{4,0},{5,7},{6,2},{7,5},{8,12},{9,11},{10,... | collective-permute-start | bytes 983048 | tf_op jit(solution)/shard_map/ppermute | solution.py:324
  50.1 0.2 collective-permute-done.9.refs_1_
  50.5 3.2 %apply_second.3 = (f32[80,512]{1,0:T(8,128)S(1)}, f32[80,512]{1,0:T(8,128)S(1)}, f32[80,1024]{1,0:T(8,128)S(1)}) custom-call(s32[3]{0:T(128)S(1)} %pad_add_fusion.place, bf16[2,80,1024]{2,1,0:T(8,128)(2,1)S(1)} %get-tuple-element.70.refs_0_, f32[80,128]{1,0:T(8,128)S(1)} %get-tuple-element.71.refs_1_, ...), custom_call_target="tpu_custom_call" | custom-call | flops 1 | bytes 1 | tf_op jit(solution)/shard_map/apply_second/pallas_call | solution.py:304
  53.7 0.5 collective-permute-start.18
  54.2 2.1 %collective-permute-start.15 = (f32[112,512]{1,0:T(8,128)S(1)}, f32[112,512]{1,0:T(8,128)S(1)}, u32[]{:S(2)}, u32[]{:S(2)}) collective-permute-start(f32[112,512]{1,0:T(8,128)S(1)} %get-tuple-element.69), channel_id=1, source_target_pairs={{0,4},{1,3},{2,6},{3,1},{4,0},{5,7},{6,2},{7,5},{8,12},{9,11},{10,... | collective-permute-start | bytes 688136 | tf_op jit(solution)/shard_map/ppermute | solution.py:324
  56.3 1.1 %collective-permute-done.16.refs_1_ = f32[80,1024]{1,0:T(8,128)S(1)} collective-permute-done((f32[80,1024]{1,0:T(8,128)S(1)}, f32[80,1024]{1,0:T(8,128)S(1)}, u32[]{:S(2)}, u32[]{:S(2)}) %collective-permute-start.16) | collective-permute-done | bytes 327712 | tf_op jit(solution)/shard_map/ppermute | solution.py:324
  57.6 3.1 %collective-permute-start.19 = (f32[80,512]{1,0:T(8,128)S(1)}, f32[80,512]{1,0:T(8,128)S(1)}, u32[]{:S(2)}, u32[]{:S(2)}) collective-permute-start(f32[80,512]{1,0:T(8,128)S(1)} %get-tuple-element.76), channel_id=1, source_target_pairs={{0,2},{1,5},{2,0},{3,7},{4,6},{5,1},{6,4},{7,3},{8,10},{9,13},{10,... | collective-permute-start | bytes 491528 | tf_op jit(solution)/shard_map/ppermute | solution.py:324
  60.7 6.6 %collective-permute-done.15 = f32[112,512]{1,0:T(8,128)S(1)} collective-permute-done((f32[112,512]{1,0:T(8,128)S(1)}, f32[112,512]{1,0:T(8,128)S(1)}, u32[]{:S(2)}, u32[]{:S(2)}) %collective-permute-start.15) | collective-permute-done | bytes 229408 | tf_op jit(solution)/shard_map/ppermute | solution.py:324
  67.3 0.8 %pad_maximum_fusion = f32[192,512]{1,0:T(8,128)} fusion(f32[80,512]{1,0:T(8,128)S(1)} %add.18, f32[112,512]{1,0:T(8,128)S(1)} %add.17), kind=kLoop, calls=%fused_computation | loop fusion | flops 98304 | bytes 786432 | tf_op jit(solution)/shard_map/concatenate | solution.py:361
  (33 shorter events, 1.3 us)
Async XLA Ops:
  0.0 8.7 %copy-start = (f32[2048]{0:T(1024)S(1)}, f32[2048]{0:T(1024)}, u32[]{:S(2)}) copy-start(f32[2048]{0:T(1024)} %param.5) | copy-start | bytes 24580
  5.6 9.5 %collective-permute-start = (f32[112,1024]{1,0:T(8,128)S(1)}, f32[112,1024]{1,0:T(8,128)S(1)}, u32[]{:S(2)}, u32[]{:S(2)}) collective-permute-start(f32[112,1024]{1,0:T(8,128)S(1)} %get-tuple-element.45), channel_id=1, source_target_pairs={{0,8},{1,17},{2,10},{3,19},{4,12},{5,21},{6,14},{7,23},{8,0},{9,25... | collective-permute-start | bytes 1376264 | tf_op jit(solution)/shard_map/ppermute | solution.py:324
  8.6 11.4 %collective-permute-start.3 = (f32[80,1024]{1,0:T(8,128)S(1)}, f32[80,1024]{1,0:T(8,128)S(1)}, u32[]{:S(2)}, u32[]{:S(2)}) collective-permute-start(f32[80,1024]{1,0:T(8,128)S(1)} %get-tuple-element.50), channel_id=1, source_target_pairs={{0,8},{1,17},{2,10},{3,19},{4,12},{5,21},{6,14},{7,23},{8,0},{9,25... | collective-permute-start | bytes 983048 | tf_op jit(solution)/shard_map/ppermute | solution.py:324
  8.7 17.2 %copy-start.1 = (f32[2048]{0:T(1024)S(1)}, f32[2048]{0:T(1024)}, u32[]{:S(2)}) copy-start(f32[2048]{0:T(1024)} %param.6) | copy-start | bytes 24580
  15.1 7.3 %collective-permute-start.1 = (f32[112,512]{1,0:T(8,128)S(1)}, f32[112,512]{1,0:T(8,128)S(1)}, u32[]{:S(2)}, u32[]{:S(2)}) collective-permute-start(f32[112,512]{1,0:T(8,128)S(1)} %get-tuple-element.47), channel_id=1, source_target_pairs={{0,16},{1,9},{2,18},{3,11},{4,20},{5,13},{6,22},{7,15},{8,24},{9,1... | collective-permute-start | bytes 688136 | tf_op jit(solution)/shard_map/ppermute | solution.py:324
  17.2 6.5 %collective-permute-start.2 = (f32[112,512]{1,0:T(8,128)S(1)}, f32[112,512]{1,0:T(8,128)S(1)}, u32[]{:S(2)}, u32[]{:S(2)}) collective-permute-start(f32[112,512]{1,0:T(8,128)S(1)} %get-tuple-element.48), channel_id=1, source_target_pairs={{0,16},{1,9},{2,18},{3,11},{4,20},{5,13},{6,22},{7,15},{8,24},{9,1... | collective-permute-start | bytes 688136 | tf_op jit(solution)/shard_map/ppermute | solution.py:324
  20.0 9.2 %collective-permute-start.6 = (f32[80,1024]{1,0:T(8,128)S(1)}, f32[80,1024]{1,0:T(8,128)S(1)}, u32[]{:S(2)}, u32[]{:S(2)}) collective-permute-start(f32[80,1024]{1,0:T(8,128)S(1)} %add_up.8.refs_3_.refs_0_), channel_id=1, source_target_pairs={{0,16},{1,9},{2,18},{3,11},{4,20},{5,13},{6,22},{7,15},{8,24},{9,1... | collective-permute-start | bytes 983048 | tf_op jit(solution)/shard_map/ppermute | solution.py:324
  23.8 6.1 %collective-permute-start.4 = (f32[112,512]{1,0:T(8,128)S(1)}, f32[112,512]{1,0:T(8,128)S(1)}, u32[]{:S(2)}, u32[]{:S(2)}) collective-permute-start(f32[112,512]{1,0:T(8,128)S(1)} %get-tuple-element.51), channel_id=1, source_target_pairs={{0,8},{1,17},{2,10},{3,19},{4,12},{5,21},{6,14},{7,23},{8,0},{9,25... | collective-permute-start | bytes 688136 | tf_op jit(solution)/shard_map/ppermute | solution.py:324
  25.8 6.5 %collective-permute-start.5 = (f32[112,512]{1,0:T(8,128)S(1)}, f32[112,512]{1,0:T(8,128)S(1)}, u32[]{:S(2)}, u32[]{:S(2)}) collective-permute-start(f32[112,512]{1,0:T(8,128)S(1)} %get-tuple-element.56), channel_id=1, source_target_pairs={{0,8},{1,17},{2,10},{3,19},{4,12},{5,21},{6,14},{7,23},{8,0},{9,25... | collective-permute-start | bytes 688136 | tf_op jit(solution)/shard_map/ppermute | solution.py:324
  34.3 2.6 %collective-permute-start.7 = (f32[112,512]{1,0:T(8,128)S(1)}, f32[112,512]{1,0:T(8,128)S(1)}, u32[]{:S(2)}, u32[]{:S(2)}) collective-permute-start(f32[112,512]{1,0:T(8,128)S(1)} %get-tuple-element.60), channel_id=1, source_target_pairs={{0,1},{1,0},{2,3},{3,2},{4,5},{5,4},{6,7},{7,6},{8,9},{9,8},{10,11... | collective-permute-start | bytes 688136 | tf_op jit(solution)/shard_map/ppermute | solution.py:324
  34.5 2.4 %collective-permute-start.8 = (f32[112,512]{1,0:T(8,128)S(1)}, f32[112,512]{1,0:T(8,128)S(1)}, u32[]{:S(2)}, u32[]{:S(2)}) collective-permute-start(f32[112,512]{1,0:T(8,128)S(1)} %get-tuple-element.61), channel_id=1, source_target_pairs={{0,1},{1,0},{2,3},{3,2},{4,5},{5,4},{6,7},{7,6},{8,9},{9,8},{10,11... | collective-permute-start | bytes 688136 | tf_op jit(solution)/shard_map/ppermute | solution.py:324
  34.9 7.1 %collective-permute-start.10 = (f32[80,1024]{1,0:T(8,128)S(1)}, f32[80,1024]{1,0:T(8,128)S(1)}, u32[]{:S(2)}, u32[]{:S(2)}) collective-permute-start(f32[80,1024]{1,0:T(8,128)S(1)} %add_up.9.refs_7_.refs_1_), channel_id=1, source_target_pairs={{0,8},{1,17},{2,10},{3,19},{4,12},{5,21},{6,14},{7,23},{8,0},{9,25... | collective-permute-start | bytes 983048 | tf_op jit(solution)/shard_map/ppermute | solution.py:324
  37.0 13.3 %collective-permute-start.9 = (f32[112,1024]{1,0:T(8,128)S(1)}, f32[112,1024]{1,0:T(8,128)S(1)}, u32[]{:S(2)}, u32[]{:S(2)}) collective-permute-start(f32[112,1024]{1,0:T(8,128)S(1)} %add_up.10.refs_4_), channel_id=1, source_target_pairs={{0,2},{1,5},{2,0},{3,7},{4,6},{5,1},{6,4},{7,3},{8,10},{9,13},{10,... | collective-permute-start | bytes 1376264 | tf_op jit(solution)/shard_map/ppermute | solution.py:324
  45.2 1.5 %collective-permute-start.11 = (f32[80,512]{1,0:T(8,128)S(1)}, f32[80,512]{1,0:T(8,128)S(1)}, u32[]{:S(2)}, u32[]{:S(2)}) collective-permute-start(f32[80,512]{1,0:T(8,128)S(1)} %get-tuple-element.64), channel_id=1, source_target_pairs={{0,1},{1,0},{2,3},{3,2},{4,5},{5,4},{6,7},{7,6},{8,9},{9,8},{10,11... | collective-permute-start | bytes 491528 | tf_op jit(solution)/shard_map/ppermute | solution.py:324
  45.3 1.6 %collective-permute-start.12 = (f32[80,512]{1,0:T(8,128)S(1)}, f32[80,512]{1,0:T(8,128)S(1)}, u32[]{:S(2)}, u32[]{:S(2)}) collective-permute-start(f32[80,512]{1,0:T(8,128)S(1)} %get-tuple-element.65), channel_id=1, source_target_pairs={{0,1},{1,0},{2,3},{3,2},{4,5},{5,4},{6,7},{7,6},{8,9},{9,8},{10,11... | collective-permute-start | bytes 491528 | tf_op jit(solution)/shard_map/ppermute | solution.py:324
  45.8 4.6 %collective-permute-start.13 = (f32[112,512]{1,0:T(8,128)S(1)}, f32[112,512]{1,0:T(8,128)S(1)}, u32[]{:S(2)}, u32[]{:S(2)}) collective-permute-start(f32[112,512]{1,0:T(8,128)S(1)} %get-tuple-element.66), channel_id=1, source_target_pairs={{0,1},{1,0},{2,3},{3,2},{4,5},{5,4},{6,7},{7,6},{8,9},{9,8},{10,11... | collective-permute-start | bytes 688136 | tf_op jit(solution)/shard_map/ppermute | solution.py:324
  45.9 4.5 %collective-permute-start.14 = (f32[112,512]{1,0:T(8,128)S(1)}, f32[112,512]{1,0:T(8,128)S(1)}, u32[]{:S(2)}, u32[]{:S(2)}) collective-permute-start(f32[112,512]{1,0:T(8,128)S(1)} %get-tuple-element.67), channel_id=1, source_target_pairs={{0,1},{1,0},{2,3},{3,2},{4,5},{5,4},{6,7},{7,6},{8,9},{9,8},{10,11... | collective-permute-start | bytes 688136 | tf_op jit(solution)/shard_map/ppermute | solution.py:324
  46.9 10.5 %collective-permute-start.16 = (f32[80,1024]{1,0:T(8,128)S(1)}, f32[80,1024]{1,0:T(8,128)S(1)}, u32[]{:S(2)}, u32[]{:S(2)}) collective-permute-start(f32[80,1024]{1,0:T(8,128)S(1)} %add_up.11.refs_2_), channel_id=1, source_target_pairs={{0,4},{1,3},{2,6},{3,1},{4,0},{5,7},{6,2},{7,5},{8,12},{9,11},{10,... | collective-permute-start | bytes 983048 | tf_op jit(solution)/shard_map/ppermute | solution.py:324
  53.7 3.8 %collective-permute-start.17 = (f32[80,512]{1,0:T(8,128)S(1)}, f32[80,512]{1,0:T(8,128)S(1)}, u32[]{:S(2)}, u32[]{:S(2)}) collective-permute-start(f32[80,512]{1,0:T(8,128)S(1)} %get-tuple-element.73), channel_id=1, source_target_pairs={{0,1},{1,0},{2,3},{3,2},{4,5},{5,4},{6,7},{7,6},{8,9},{9,8},{10,11... | collective-permute-start | bytes 491528 | tf_op jit(solution)/shard_map/ppermute | solution.py:324
  53.7 3.8 %collective-permute-start.18 = (f32[80,512]{1,0:T(8,128)S(1)}, f32[80,512]{1,0:T(8,128)S(1)}, u32[]{:S(2)}, u32[]{:S(2)}) collective-permute-start(f32[80,512]{1,0:T(8,128)S(1)} %get-tuple-element.74), channel_id=1, source_target_pairs={{0,1},{1,0},{2,3},{3,2},{4,5},{5,4},{6,7},{7,6},{8,9},{9,8},{10,11... | collective-permute-start | bytes 491528 | tf_op jit(solution)/shard_map/ppermute | solution.py:324
  54.2 13.0 %collective-permute-start.15 = (f32[112,512]{1,0:T(8,128)S(1)}, f32[112,512]{1,0:T(8,128)S(1)}, u32[]{:S(2)}, u32[]{:S(2)}) collective-permute-start(f32[112,512]{1,0:T(8,128)S(1)} %get-tuple-element.69), channel_id=1, source_target_pairs={{0,4},{1,3},{2,6},{3,1},{4,0},{5,7},{6,2},{7,5},{8,12},{9,11},{10,... | collective-permute-start | bytes 688136 | tf_op jit(solution)/shard_map/ppermute | solution.py:324
  57.6 9.7 %collective-permute-start.19 = (f32[80,512]{1,0:T(8,128)S(1)}, f32[80,512]{1,0:T(8,128)S(1)}, u32[]{:S(2)}, u32[]{:S(2)}) collective-permute-start(f32[80,512]{1,0:T(8,128)S(1)} %get-tuple-element.76), channel_id=1, source_target_pairs={{0,2},{1,5},{2,0},{3,7},{4,6},{5,1},{6,4},{7,3},{8,10},{9,13},{10,... | collective-permute-start | bytes 491528 | tf_op jit(solution)/shard_map/ppermute | solution.py:324

commit v5 on v4

--- a/solution.py
+++ b/solution.py
@@ -73,13 +73,13 @@
         else:
             left = probes[:, at]
         right = held[slot, at]
+        product = jnp.dot(left, right, preferred_element_type=F32)
         low = 0
         for part, many in zip(parts, CHUNKS):
-            product = jnp.dot(left[low : low + many], right, preferred_element_type=F32)
             if step == 0:
-                part[...] = product
+                part[...] = product[low : low + many]
             else:
-                part[...] += product
+                part[...] += product[low : low + many]
             low += many
     if first:
         sums[...] = jnp.broadcast_to(total, sums.shape)

time: 68.2 us -> 68.2 us (level)
  no operation moved by 1% of the time
where the time goes in v5:
time: 68.2 us; the launch traced here: 68 us
  Pallas kernels  24.1 us (35%)
  starting transfers between devices  24 us (35%)
  waiting for transfers between devices  18.8 us (28%)
  other arithmetic  0.91 us (1%)
    ppermute x20, starting transfers between devices, on_slice(): send = lambda array, moves: lax.ppermute(array, AXES, moves)  24 us
    ppermute x20, waiting for transfers between devices, on_slice(): send = lambda array, moves: lax.ppermute(array, AXES, moves)  18.8 us
    pallas_call x4, Pallas kernels, apply_rows(): pl.pallas_call(functools.partial(apply_kernel, first, split, swapped, fac...  10.5 us
    pallas_call x1, Pallas kernels, first_half(): pl.pallas_call(functools.partial(loads_kernel, True), in_specs=[SMEM, HBM...  5.41 us
    pallas_call x1, Pallas kernels, second_half(): pl.pallas_call(functools.partial(loads_kernel, False), in_specs=[SMEM, VM...  4.41 us
    pallas_call x1, Pallas kernels, own_rows(): pl.pallas_call(functools.partial(own_kernel, swapped, factor), in_specs=[...  3.33 us
  transfers between devices with their start and end apart: 20, of which 11 were waited for; matrix products, arithmetic and copies ran while one was open for 0% of the time, Pallas kernels for 25%

profile of v5, /device:TPU:0, one launch (start us, length us, event | category | flops | bytes accessed | tf_op | source)
XLA Modules:
  0.0 68.0 jit_solution(6203270604287818659)
XLA Ops:
  0.1 5.4 %loads_sent.1 = (f32[112,1024]{1,0:T(8,128)S(1)}, f32[80,1024]{1,0:T(8,128)S(1)}, bf16[192,4096]{1,0:T(8,128)(2,1)S(1)}, f32[192,128]{1,0:T(8,128)S(1)}, bf16[2,4096,1024]{2,1,0:T(8,128)(2,1)S(1)}) custom-call(s32[3]{0:T(128)S(1)} %pad_add_fusion.place, f32[192,4096]{1,0:T(8,128)} %probes.1, bf16[4096,2048]{1,0:T(8,128)(2,1)} %dosage.3, f32[1,2048]{1,0:T(1,128)} %bitcast.5), custom_call_target="tpu_custom_call" | custom-call | flops 1 | bytes 1 | tf_op jit(solution)/shard_map/loads_sent/pallas_call | solution.py:108
  5.5 3.0 %collective-permute-start = (f32[112,1024]{1,0:T(8,128)S(1)}, f32[112,1024]{1,0:T(8,128)S(1)}, u32[]{:S(2)}, u32[]{:S(2)}) collective-permute-start(f32[112,1024]{1,0:T(8,128)S(1)} %get-tuple-element.45), channel_id=1, source_target_pairs={{0,8},{1,17},{2,10},{3,19},{4,12},{5,21},{6,14},{7,23},{8,0},{9,25... | collective-permute-start | bytes 1376264 | tf_op jit(solution)/shard_map/ppermute | solution.py:324
  8.6 4.4 %loads_kept.1 = (f32[112,1024]{1,0:T(8,128)S(1)}, f32[80,1024]{1,0:T(8,128)S(1)}, bf16[2,4096,1024]{2,1,0:T(8,128)(2,1)S(1)}) custom-call(s32[3]{0:T(128)S(1)} %pad_add_fusion.place, bf16[192,4096]{1,0:T(8,128)(2,1)S(1)} %get-tuple-element.41.probes, bf16[4096,2048]{1,0:T(8,128)(2,1)} %dosage.3, ...), custom_call_target="tpu_custom_call", output_to_operand_aliasing={{2}: (5, {})} | custom-call | flops 1 | bytes 1 | tf_op jit(solution)/shard_map/loads_kept/pallas_call | solution.py:134
  13.0 2.0 %collective-permute-done.refs_1_ = f32[112,1024]{1,0:T(8,128)S(1)} collective-permute-done((f32[112,1024]{1,0:T(8,128)S(1)}, f32[112,1024]{1,0:T(8,128)S(1)}, u32[]{:S(2)}, u32[]{:S(2)}) %collective-permute-start) | collective-permute-done | bytes 458784 | tf_op jit(solution)/shard_map/ppermute | solution.py:324
  15.0 2.1 %collective-permute-start.1 = (f32[112,512]{1,0:T(8,128)S(1)}, f32[112,512]{1,0:T(8,128)S(1)}, u32[]{:S(2)}, u32[]{:S(2)}) collective-permute-start(f32[112,512]{1,0:T(8,128)S(1)} %get-tuple-element.47), channel_id=1, source_target_pairs={{0,16},{1,9},{2,18},{3,11},{4,20},{5,13},{6,22},{7,15},{8,24},{9,1... | collective-permute-start | bytes 688136 | tf_op jit(solution)/shard_map/ppermute | solution.py:324
  17.2 2.7 %collective-permute-done.3.refs_1_ = f32[80,1024]{1,0:T(8,128)S(1)} collective-permute-done((f32[80,1024]{1,0:T(8,128)S(1)}, f32[80,1024]{1,0:T(8,128)S(1)}, u32[]{:S(2)}, u32[]{:S(2)}) %collective-permute-start.3) | collective-permute-done | bytes 327712 | tf_op jit(solution)/shard_map/ppermute | solution.py:324
  20.0 2.4 %collective-permute-start.6 = (f32[80,1024]{1,0:T(8,128)S(1)}, f32[80,1024]{1,0:T(8,128)S(1)}, u32[]{:S(2)}, u32[]{:S(2)}) collective-permute-start(f32[80,1024]{1,0:T(8,128)S(1)} %add_up.8.refs_3_.refs_0_), channel_id=1, source_target_pairs={{0,16},{1,9},{2,18},{3,11},{4,20},{5,13},{6,22},{7,15},{8,24},{9,1... | collective-permute-start | bytes 983048 | tf_op jit(solution)/shard_map/ppermute | solution.py:324
  22.4 1.2 %collective-permute-done.2.refs_2_ = f32[112,512]{1,0:T(8,128)S(1)} collective-permute-done((f32[112,512]{1,0:T(8,128)S(1)}, f32[112,512]{1,0:T(8,128)S(1)}, u32[]{:S(2)}, u32[]{:S(2)}) %collective-permute-start.2) | collective-permute-done | bytes 229408 | tf_op jit(solution)/shard_map/ppermute | solution.py:324
  23.7 2.1 %collective-permute-start.4 = (f32[112,512]{1,0:T(8,128)S(1)}, f32[112,512]{1,0:T(8,128)S(1)}, u32[]{:S(2)}, u32[]{:S(2)}) collective-permute-start(f32[112,512]{1,0:T(8,128)S(1)} %get-tuple-element.51), channel_id=1, source_target_pairs={{0,8},{1,17},{2,10},{3,19},{4,12},{5,21},{6,14},{7,23},{8,0},{9,25... | collective-permute-start | bytes 688136 | tf_op jit(solution)/shard_map/ppermute | solution.py:324
  25.8 3.3 %own_rows.1 = (f32[112,4096]{1,0:T(8,128)S(1)}, f32[112,128]{1,0:T(8,128)S(1)}) custom-call(s32[3]{0:T(128)S(1)} %pad_add_fusion.place, f32[112,1024]{1,0:T(8,128)S(1)} %get-tuple-element.52.own, f32[1,2048]{1,0:T(1,128)S(1)} %bitcast.7, f32[1,2048]{1,0:T(1,128)S(1)} %bitcast.10, bf16[2,4096,1024]{2,1,0:T(8,128)(2,1)S(1)} %get-tuple-element.53.held.refs_4_.refs_2_), custom_call_target="tpu_custom_call" | custom-call | flops 1 | bytes 1 | tf_op jit(solution)/shard_map/own_rows/pallas_call | solution.py:282
  29.2 0.5 collective-permute-done.4.refs_0_
  29.8 2.5 %collective-permute-done.5.refs_6_ = f32[112,512]{1,0:T(8,128)S(1)} collective-permute-done((f32[112,512]{1,0:T(8,128)S(1)}, f32[112,512]{1,0:T(8,128)S(1)}, u32[]{:S(2)}, u32[]{:S(2)}) %collective-permute-start.5) | collective-permute-done | bytes 229408 | tf_op jit(solution)/shard_map/ppermute | solution.py:324
  32.2 2.0 %apply_first.2 = (f32[112,512]{1,0:T(8,128)S(1)}, f32[112,512]{1,0:T(8,128)S(1)}, f32[112,1024]{1,0:T(8,128)S(1)}, bf16[1,112,1024]{2,1,0:T(8,128)(2,1)S(1)}, f32[112,128]{1,0:T(8,128)S(1)}) custom-call(s32[3]{0:T(128)S(1)} %pad_add_fusion.place, f32[112,512]{1,0:T(8,128)S(1)} %collective-permute-done.4.refs_0_, ...), custom_call_target="tpu_custom_call" | custom-call | flops 1 | bytes 1 | tf_op jit(solution)/shard_map/apply_first/pallas_call | solution.py:304
  34.4 0.4 collective-permute-start.8
  34.8 2.0 %collective-permute-start.10 = (f32[80,1024]{1,0:T(8,128)S(1)}, f32[80,1024]{1,0:T(8,128)S(1)}, u32[]{:S(2)}, u32[]{:S(2)}) collective-permute-start(f32[80,1024]{1,0:T(8,128)S(1)} %add_up.9.refs_7_.refs_1_), channel_id=1, source_target_pairs={{0,8},{1,17},{2,10},{3,19},{4,12},{5,21},{6,14},{7,23},{8,0},{9,25... | collective-permute-start | bytes 983048 | tf_op jit(solution)/shard_map/ppermute | solution.py:324
  36.9 1.6 %collective-permute-start.9 = (f32[112,1024]{1,0:T(8,128)S(1)}, f32[112,1024]{1,0:T(8,128)S(1)}, u32[]{:S(2)}, u32[]{:S(2)}) collective-permute-start(f32[112,1024]{1,0:T(8,128)S(1)} %add_up.10.refs_4_), channel_id=1, source_target_pairs={{0,2},{1,5},{2,0},{3,7},{4,6},{5,1},{6,4},{7,3},{8,10},{9,13},{10,... | collective-permute-start | bytes 1376264 | tf_op jit(solution)/shard_map/ppermute | solution.py:324
  38.5 2.0 %apply_second.2 = (f32[112,512]{1,0:T(8,128)S(1)}, f32[112,512]{1,0:T(8,128)S(1)}, f32[112,1024]{1,0:T(8,128)S(1)}) custom-call(s32[3]{0:T(128)S(1)} %pad_add_fusion.place, bf16[1,112,1024]{2,1,0:T(8,128)(2,1)S(1)} %get-tuple-element.57.refs_0_, f32[112,128]{1,0:T(8,128)S(1)} %get-tuple-element.58.refs_1_, ...), custom_call_target="tpu_custom_call" | custom-call | flops 1 | bytes 1 | tf_op jit(solution)/shard_map/apply_second/pallas_call | solution.py:304
  40.6 1.3 %collective-permute-done.10.refs_0_ = f32[80,1024]{1,0:T(8,128)S(1)} collective-permute-done((f32[80,1024]{1,0:T(8,128)S(1)}, f32[80,1024]{1,0:T(8,128)S(1)}, u32[]{:S(2)}, u32[]{:S(2)}) %collective-permute-start.10) | collective-permute-done | bytes 327712 | tf_op jit(solution)/shard_map/ppermute | solution.py:324
  41.9 3.2 %apply_first.3 = (f32[80,512]{1,0:T(8,128)S(1)}, f32[80,512]{1,0:T(8,128)S(1)}, f32[80,1024]{1,0:T(8,128)S(1)}, bf16[2,80,1024]{2,1,0:T(8,128)(2,1)S(1)}, f32[80,128]{1,0:T(8,128)S(1)}) custom-call(s32[3]{0:T(128)S(1)} %pad_add_fusion.place, f32[80,1024]{1,0:T(8,128)S(1)} %collective-permute-done.10.refs_0_, f32[80,1024]{1,0:T(8,128)S(1)} %add_up.9.refs_7_.refs_1_, ...), custom_call_target="tpu_custom_call" | custom-call | flops 1 | bytes 1 | tf_op jit(solution)/shard_map/apply_first/pallas_call | solution.py:304
  45.2 0.5 collective-permute-start.12
  45.8 0.4 collective-permute-start.14
  46.2 0.4 collective-permute-done.11.refs_1_
  46.6 0.2 collective-permute-done.12.refs_2_
  46.8 3.2 %collective-permute-start.16 = (f32[80,1024]{1,0:T(8,128)S(1)}, f32[80,1024]{1,0:T(8,128)S(1)}, u32[]{:S(2)}, u32[]{:S(2)}) collective-permute-start(f32[80,1024]{1,0:T(8,128)S(1)} %add_up.11.refs_2_), channel_id=1, source_target_pairs={{0,4},{1,3},{2,6},{3,1},{4,0},{5,7},{6,2},{7,5},{8,12},{9,11},{10,... | collective-permute-start | bytes 983048 | tf_op jit(solution)/shard_map/ppermute | solution.py:324
  50.0 0.2 collective-permute-done.9.refs_1_
  50.4 3.2 %apply_second.3 = (f32[80,512]{1,0:T(8,128)S(1)}, f32[80,512]{1,0:T(8,128)S(1)}, f32[80,1024]{1,0:T(8,128)S(1)}) custom-call(s32[3]{0:T(128)S(1)} %pad_add_fusion.place, bf16[2,80,1024]{2,1,0:T(8,128)(2,1)S(1)} %get-tuple-element.70.refs_0_, f32[80,128]{1,0:T(8,128)S(1)} %get-tuple-element.71.refs_1_, ...), custom_call_target="tpu_custom_call" | custom-call | flops 1 | bytes 1 | tf_op jit(solution)/shard_map/apply_second/pallas_call | solution.py:304
  53.7 0.5 collective-permute-start.18
  54.2 2.1 %collective-permute-start.15 = (f32[112,512]{1,0:T(8,128)S(1)}, f32[112,512]{1,0:T(8,128)S(1)}, u32[]{:S(2)}, u32[]{:S(2)}) collective-permute-start(f32[112,512]{1,0:T(8,128)S(1)} %get-tuple-element.69), channel_id=1, source_target_pairs={{0,4},{1,3},{2,6},{3,1},{4,0},{5,7},{6,2},{7,5},{8,12},{9,11},{10,... | collective-permute-start | bytes 688136 | tf_op jit(solution)/shard_map/ppermute | solution.py:324
  56.2 1.1 %collective-permute-done.16.refs_1_ = f32[80,1024]{1,0:T(8,128)S(1)} collective-permute-done((f32[80,1024]{1,0:T(8,128)S(1)}, f32[80,1024]{1,0:T(8,128)S(1)}, u32[]{:S(2)}, u32[]{:S(2)}) %collective-permute-start.16) | collective-permute-done | bytes 327712 | tf_op jit(solution)/shard_map/ppermute | solution.py:324
  57.5 3.1 %collective-permute-start.19 = (f32[80,512]{1,0:T(8,128)S(1)}, f32[80,512]{1,0:T(8,128)S(1)}, u32[]{:S(2)}, u32[]{:S(2)}) collective-permute-start(f32[80,512]{1,0:T(8,128)S(1)} %get-tuple-element.76), channel_id=1, source_target_pairs={{0,2},{1,5},{2,0},{3,7},{4,6},{5,1},{6,4},{7,3},{8,10},{9,13},{10,... | collective-permute-start | bytes 491528 | tf_op jit(solution)/shard_map/ppermute | solution.py:324
  60.6 6.6 %collective-permute-done.15 = f32[112,512]{1,0:T(8,128)S(1)} collective-permute-done((f32[112,512]{1,0:T(8,128)S(1)}, f32[112,512]{1,0:T(8,128)S(1)}, u32[]{:S(2)}, u32[]{:S(2)}) %collective-permute-start.15) | collective-permute-done | bytes 229408 | tf_op jit(solution)/shard_map/ppermute | solution.py:324
  67.3 0.8 %pad_maximum_fusion = f32[192,512]{1,0:T(8,128)} fusion(f32[80,512]{1,0:T(8,128)S(1)} %add.18, f32[112,512]{1,0:T(8,128)S(1)} %add.17), kind=kLoop, calls=%fused_computation | loop fusion | flops 98304 | bytes 786432 | tf_op jit(solution)/shard_map/concatenate | solution.py:361
  (33 shorter events, 1.3 us)
Async XLA Ops:
  0.0 8.6 %copy-start = (f32[2048]{0:T(1024)S(1)}, f32[2048]{0:T(1024)}, u32[]{:S(2)}) copy-start(f32[2048]{0:T(1024)} %param.5) | copy-start | bytes 24580
  5.5 9.5 %collective-permute-start = (f32[112,1024]{1,0:T(8,128)S(1)}, f32[112,1024]{1,0:T(8,128)S(1)}, u32[]{:S(2)}, u32[]{:S(2)}) collective-permute-start(f32[112,1024]{1,0:T(8,128)S(1)} %get-tuple-element.45), channel_id=1, source_target_pairs={{0,8},{1,17},{2,10},{3,19},{4,12},{5,21},{6,14},{7,23},{8,0},{9,25... | collective-permute-start | bytes 1376264 | tf_op jit(solution)/shard_map/ppermute | solution.py:324
  8.5 11.4 %collective-permute-start.3 = (f32[80,1024]{1,0:T(8,128)S(1)}, f32[80,1024]{1,0:T(8,128)S(1)}, u32[]{:S(2)}, u32[]{:S(2)}) collective-permute-start(f32[80,1024]{1,0:T(8,128)S(1)} %get-tuple-element.50), channel_id=1, source_target_pairs={{0,8},{1,17},{2,10},{3,19},{4,12},{5,21},{6,14},{7,23},{8,0},{9,25... | collective-permute-start | bytes 983048 | tf_op jit(solution)/shard_map/ppermute | solution.py:324
  8.6 17.2 %copy-start.1 = (f32[2048]{0:T(1024)S(1)}, f32[2048]{0:T(1024)}, u32[]{:S(2)}) copy-start(f32[2048]{0:T(1024)} %param.6) | copy-start | bytes 24580
  15.0 7.3 %collective-permute-start.1 = (f32[112,512]{1,0:T(8,128)S(1)}, f32[112,512]{1,0:T(8,128)S(1)}, u32[]{:S(2)}, u32[]{:S(2)}) collective-permute-start(f32[112,512]{1,0:T(8,128)S(1)} %get-tuple-element.47), channel_id=1, source_target_pairs={{0,16},{1,9},{2,18},{3,11},{4,20},{5,13},{6,22},{7,15},{8,24},{9,1... | collective-permute-start | bytes 688136 | tf_op jit(solution)/shard_map/ppermute | solution.py:324
  17.1 6.5 %collective-permute-start.2 = (f32[112,512]{1,0:T(8,128)S(1)}, f32[112,512]{1,0:T(8,128)S(1)}, u32[]{:S(2)}, u32[]{:S(2)}) collective-permute-start(f32[112,512]{1,0:T(8,128)S(1)} %get-tuple-element.48), channel_id=1, source_target_pairs={{0,16},{1,9},{2,18},{3,11},{4,20},{5,13},{6,22},{7,15},{8,24},{9,1... | collective-permute-start | bytes 688136 | tf_op jit(solution)/shard_map/ppermute | solution.py:324
  20.0 9.2 %collective-permute-start.6 = (f32[80,1024]{1,0:T(8,128)S(1)}, f32[80,1024]{1,0:T(8,128)S(1)}, u32[]{:S(2)}, u32[]{:S(2)}) collective-permute-start(f32[80,1024]{1,0:T(8,128)S(1)} %add_up.8.refs_3_.refs_0_), channel_id=1, source_target_pairs={{0,16},{1,9},{2,18},{3,11},{4,20},{5,13},{6,22},{7,15},{8,24},{9,1... | collective-permute-start | bytes 983048 | tf_op jit(solution)/shard_map/ppermute | solution.py:324
  23.7 6.1 %collective-permute-start.4 = (f32[112,512]{1,0:T(8,128)S(1)}, f32[112,512]{1,0:T(8,128)S(1)}, u32[]{:S(2)}, u32[]{:S(2)}) collective-permute-start(f32[112,512]{1,0:T(8,128)S(1)} %get-tuple-element.51), channel_id=1, source_target_pairs={{0,8},{1,17},{2,10},{3,19},{4,12},{5,21},{6,14},{7,23},{8,0},{9,25... | collective-permute-start | bytes 688136 | tf_op jit(solution)/shard_map/ppermute | solution.py:324
  25.7 6.5 %collective-permute-start.5 = (f32[112,512]{1,0:T(8,128)S(1)}, f32[112,512]{1,0:T(8,128)S(1)}, u32[]{:S(2)}, u32[]{:S(2)}) collective-permute-start(f32[112,512]{1,0:T(8,128)S(1)} %get-tuple-element.56), channel_id=1, source_target_pairs={{0,8},{1,17},{2,10},{3,19},{4,12},{5,21},{6,14},{7,23},{8,0},{9,25... | collective-permute-start | bytes 688136 | tf_op jit(solution)/shard_map/ppermute | solution.py:324
  34.2 2.6 %collective-permute-start.7 = (f32[112,512]{1,0:T(8,128)S(1)}, f32[112,512]{1,0:T(8,128)S(1)}, u32[]{:S(2)}, u32[]{:S(2)}) collective-permute-start(f32[112,512]{1,0:T(8,128)S(1)} %get-tuple-element.60), channel_id=1, source_target_pairs={{0,1},{1,0},{2,3},{3,2},{4,5},{5,4},{6,7},{7,6},{8,9},{9,8},{10,11... | collective-permute-start | bytes 688136 | tf_op jit(solution)/shard_map/ppermute | solution.py:324
  34.4 2.4 %collective-permute-start.8 = (f32[112,512]{1,0:T(8,128)S(1)}, f32[112,512]{1,0:T(8,128)S(1)}, u32[]{:S(2)}, u32[]{:S(2)}) collective-permute-start(f32[112,512]{1,0:T(8,128)S(1)} %get-tuple-element.61), channel_id=1, source_target_pairs={{0,1},{1,0},{2,3},{3,2},{4,5},{5,4},{6,7},{7,6},{8,9},{9,8},{10,11... | collective-permute-start | bytes 688136 | tf_op jit(solution)/shard_map/ppermute | solution.py:324
  34.8 7.1 %collective-permute-start.10 = (f32[80,1024]{1,0:T(8,128)S(1)}, f32[80,1024]{1,0:T(8,128)S(1)}, u32[]{:S(2)}, u32[]{:S(2)}) collective-permute-start(f32[80,1024]{1,0:T(8,128)S(1)} %add_up.9.refs_7_.refs_1_), channel_id=1, source_target_pairs={{0,8},{1,17},{2,10},{3,19},{4,12},{5,21},{6,14},{7,23},{8,0},{9,25... | collective-permute-start | bytes 983048 | tf_op jit(solution)/shard_map/ppermute | solution.py:324
  36.9 13.3 %collective-permute-start.9 = (f32[112,1024]{1,0:T(8,128)S(1)}, f32[112,1024]{1,0:T(8,128)S(1)}, u32[]{:S(2)}, u32[]{:S(2)}) collective-permute-start(f32[112,1024]{1,0:T(8,128)S(1)} %add_up.10.refs_4_), channel_id=1, source_target_pairs={{0,2},{1,5},{2,0},{3,7},{4,6},{5,1},{6,4},{7,3},{8,10},{9,13},{10,... | collective-permute-start | bytes 1376264 | tf_op jit(solution)/shard_map/ppermute | solution.py:324
  45.1 1.5 %collective-permute-start.11 = (f32[80,512]{1,0:T(8,128)S(1)}, f32[80,512]{1,0:T(8,128)S(1)}, u32[]{:S(2)}, u32[]{:S(2)}) collective-permute-start(f32[80,512]{1,0:T(8,128)S(1)} %get-tuple-element.64), channel_id=1, source_target_pairs={{0,1},{1,0},{2,3},{3,2},{4,5},{5,4},{6,7},{7,6},{8,9},{9,8},{10,11... | collective-permute-start | bytes 491528 | tf_op jit(solution)/shard_map/ppermute | solution.py:324
  45.2 1.6 %collective-permute-start.12 = (f32[80,512]{1,0:T(8,128)S(1)}, f32[80,512]{1,0:T(8,128)S(1)}, u32[]{:S(2)}, u32[]{:S(2)}) collective-permute-start(f32[80,512]{1,0:T(8,128)S(1)} %get-tuple-element.65), channel_id=1, source_target_pairs={{0,1},{1,0},{2,3},{3,2},{4,5},{5,4},{6,7},{7,6},{8,9},{9,8},{10,11... | collective-permute-start | bytes 491528 | tf_op jit(solution)/shard_map/ppermute | solution.py:324
  45.7 4.6 %collective-permute-start.13 = (f32[112,512]{1,0:T(8,128)S(1)}, f32[112,512]{1,0:T(8,128)S(1)}, u32[]{:S(2)}, u32[]{:S(2)}) collective-permute-start(f32[112,512]{1,0:T(8,128)S(1)} %get-tuple-element.66), channel_id=1, source_target_pairs={{0,1},{1,0},{2,3},{3,2},{4,5},{5,4},{6,7},{7,6},{8,9},{9,8},{10,11... | collective-permute-start | bytes 688136 | tf_op jit(solution)/shard_map/ppermute | solution.py:324
  45.8 4.5 %collective-permute-start.14 = (f32[112,512]{1,0:T(8,128)S(1)}, f32[112,512]{1,0:T(8,128)S(1)}, u32[]{:S(2)}, u32[]{:S(2)}) collective-permute-start(f32[112,512]{1,0:T(8,128)S(1)} %get-tuple-element.67), channel_id=1, source_target_pairs={{0,1},{1,0},{2,3},{3,2},{4,5},{5,4},{6,7},{7,6},{8,9},{9,8},{10,11... | collective-permute-start | bytes 688136 | tf_op jit(solution)/shard_map/ppermute | solution.py:324
  46.8 10.5 %collective-permute-start.16 = (f32[80,1024]{1,0:T(8,128)S(1)}, f32[80,1024]{1,0:T(8,128)S(1)}, u32[]{:S(2)}, u32[]{:S(2)}) collective-permute-start(f32[80,1024]{1,0:T(8,128)S(1)} %add_up.11.refs_2_), channel_id=1, source_target_pairs={{0,4},{1,3},{2,6},{3,1},{4,0},{5,7},{6,2},{7,5},{8,12},{9,11},{10,... | collective-permute-start | bytes 983048 | tf_op jit(solution)/shard_map/ppermute | solution.py:324
  53.6 3.8 %collective-permute-start.17 = (f32[80,512]{1,0:T(8,128)S(1)}, f32[80,512]{1,0:T(8,128)S(1)}, u32[]{:S(2)}, u32[]{:S(2)}) collective-permute-start(f32[80,512]{1,0:T(8,128)S(1)} %get-tuple-element.73), channel_id=1, source_target_pairs={{0,1},{1,0},{2,3},{3,2},{4,5},{5,4},{6,7},{7,6},{8,9},{9,8},{10,11... | collective-permute-start | bytes 491528 | tf_op jit(solution)/shard_map/ppermute | solution.py:324
  53.7 3.8 %collective-permute-start.18 = (f32[80,512]{1,0:T(8,128)S(1)}, f32[80,512]{1,0:T(8,128)S(1)}, u32[]{:S(2)}, u32[]{:S(2)}) collective-permute-start(f32[80,512]{1,0:T(8,128)S(1)} %get-tuple-element.74), channel_id=1, source_target_pairs={{0,1},{1,0},{2,3},{3,2},{4,5},{5,4},{6,7},{7,6},{8,9},{9,8},{10,11... | collective-permute-start | bytes 491528 | tf_op jit(solution)/shard_map/ppermute | solution.py:324
  54.2 13.0 %collective-permute-start.15 = (f32[112,512]{1,0:T(8,128)S(1)}, f32[112,512]{1,0:T(8,128)S(1)}, u32[]{:S(2)}, u32[]{:S(2)}) collective-permute-start(f32[112,512]{1,0:T(8,128)S(1)} %get-tuple-element.69), channel_id=1, source_target_pairs={{0,4},{1,3},{2,6},{3,1},{4,0},{5,7},{6,2},{7,5},{8,12},{9,11},{10,... | collective-permute-start | bytes 688136 | tf_op jit(solution)/shard_map/ppermute | solution.py:324
  57.5 9.7 %collective-permute-start.19 = (f32[80,512]{1,0:T(8,128)S(1)}, f32[80,512]{1,0:T(8,128)S(1)}, u32[]{:S(2)}, u32[]{:S(2)}) collective-permute-start(f32[80,512]{1,0:T(8,128)S(1)} %get-tuple-element.76), channel_id=1, source_target_pairs={{0,2},{1,5},{2,0},{3,7},{4,6},{5,1},{6,4},{7,3},{8,10},{9,13},{10,... | collective-permute-start | bytes 491528 | tf_op jit(solution)/shard_map/ppermute | solution.py:324
